TPU v7x, 512 devices: a whole 4x4x16 slice. The times are simulated.
512 devices in a mesh: gx: 32 (over z, y_hi), gy: 16 (over x, y_lo, core).
Axes of the slice: x: 4, y: 4 (y_hi: 2, y_lo: 2; y = y_hi * 2 + y_lo), z: 16, core: 2. Of those that a mesh axis runs over, the one named last changes fastest.
Arguments:
- disp: float32 [2, 1024, 2048], P(None, 'gx', 'gy'), may hold values from -0.1 to 0.1
- vel: float32 [2, 1024, 2048], P(None, 'gx', 'gy'), may hold values from -1.5 to 1.5
- stiffness: float32 [1024, 2048], P('gx', 'gy'), may hold values from 2 to 20
- body_force: float32 [2, 1024, 2048], P(None, 'gx', 'gy'), may hold values from -6 to 6
- bond_bits: int32 [2, 1024, 2048], P(None, 'gx', 'gy'), may hold values from 0 to 16383, as said below
Outputs:
- disp_final: float32 [2, 1024, 2048], P(None, 'gx', 'gy')
- vel_final: float32 [2, 1024, 2048], P(None, 'gx', 'gy')
Inputs may be any that keep to these rules, and one draw needn't show every extreme that they name: `bond_bits`: bit j of word 0 of a point (j below 14) is 1 where its bond to offset j of the upper shell exists, bit j of word 1 where its bond to the mirrored offset exists; both ends of a bond carry the same flag, bonds that leave the plate are absent, and bits 14 and above are 0.
All inputs are finite; a program needn't handle non-finite values.
Results may differ from a plain program's by a relative error of at most 0.000026.
Values sent between devices are 32-bit elements; how exact they have to be, the bound alone decides.
A program may use at most 64 MiB of HBM per device.

v0:
```python
import math

import jax
import jax.numpy as jnp
from jax import lax
from jax.sharding import PartitionSpec as P

STEPS = 10


TIME_STEP = 0.04


def extended_2(block, sides, width):
    for axis, dim in sides:
        count = lax.axis_size(axis)
        forward = [(i, i + 1) for i in range(count - 1)]
        backward = [(target, source) for source, target in forward]
        low = lax.ppermute(
            lax.slice_in_dim(block, block.shape[dim] - width, None, axis=dim), axis, forward
        )
        high = lax.ppermute(lax.slice_in_dim(block, 0, width, axis=dim), axis, backward)
        block = jnp.concatenate([low, block, high], axis=dim)
    return block


def shell_offsets():
    upper = []
    for row_step in range(0, 4):
        for col_step in range(-3, 4):
            if row_step * row_step + col_step * col_step <= 9 and (row_step > 0 or col_step > 0):
                upper.append((row_step, col_step))
    return upper


def bond_term(itself, other, offset, bond_bits, index):
    row_step, col_step = offset
    spread_x = row_step + other[0] - itself[0]
    spread_y = col_step + other[1] - itself[1]
    length = math.sqrt(row_step * row_step + col_step * col_step)
    dist = jnp.sqrt(spread_x * spread_x + spread_y * spread_y)
    live = bond_bits[index // 14] // 2 ** (index % 14) % 2
    weight = 0.5 * (itself[2] + other[2]) * (dist - length) / (length * dist)
    weight = jnp.where(live == 1, weight, jnp.zeros_like(weight))
    return (weight * spread_x, weight * spread_y)


def import_rims(fields):
    extended = extended_2(fields, (("gx", 1), ("gy", 2)), 3)
    return extended


def full_forces(fields, moving, bond_bits):
    rows_own, cols_own = (fields.shape[1], fields.shape[2])
    extended = import_rims(moving)
    itself = (fields[0], fields[1], fields[2])
    upper = shell_offsets()
    offsets = upper + [(-row_step, -col_step) for row_step, col_step in upper]
    force_x = jnp.zeros((rows_own, cols_own), jnp.float32)
    force_y = jnp.zeros((rows_own, cols_own), jnp.float32)
    for index, (row_step, col_step) in enumerate(offsets):
        window = extended[
            :, 3 + row_step : 3 + row_step + rows_own, 3 + col_step : 3 + col_step + cols_own
        ]
        other = (window[0], window[1], window[2])
        term_x, term_y = bond_term(itself, other, (row_step, col_step), bond_bits, index)
        force_x = force_x + term_x
        force_y = force_y + term_y
    return jnp.stack([force_x, force_y])


def on_device(disp, vel, stiffness, body_force, bond_bits):

    def accelerate(current):
        fields = jnp.concatenate([current, stiffness[None]], axis=0)
        forces = full_forces(fields, fields, bond_bits)
        return forces + body_force

    def advance(step, carry):
        current, velocity, accel = carry
        halfway = velocity + 0.5 * TIME_STEP * accel
        current = current + TIME_STEP * halfway
        accel = accelerate(current)
        return (current, halfway + 0.5 * TIME_STEP * accel, accel)

    start = accelerate(disp)
    final_disp, final_vel, last_accel = lax.fori_loop(0, STEPS, advance, (disp, vel, start))
    return (final_disp, final_vel)


def solution(mesh):
    in_specs = (
        P(None, "gx", "gy"),
        P(None, "gx", "gy"),
        P("gx", "gy"),
        P(None, "gx", "gy"),
        P(None, "gx", "gy"),
    )
    out_specs = (P(None, "gx", "gy"), P(None, "gx", "gy"))
    return jax.shard_map(
        on_device, mesh=mesh, in_specs=in_specs, out_specs=out_specs, check_vma=False
    )
```

profile of v0, /device:TPU:397, one launch (start us, length us, event | category | flops | bytes accessed | tf_op | source)
XLA Modules:
  0.0 246.1 jit_solution(9236118208381251626)
XLA Ops:
  2.1 4.0 %collective-permute-start.4 = (f32[3,3,128]{2,1,0:T(4,128)S(1)}, f32[3,3,128]{2,1,0:T(4,128)S(1)}, u32[]{:S(2)}, u32[]{:S(2)}) collective-permute-start(f32[3,3,128]{2,1,0:T(4,128)S(1)} %get-tuple-element.542), channel_id=1, source_target_pairs={{0,16},{16,32},{32,48},{48,64},{64,80},{80,96},{96,112},{112,128},... | collective-permute-start | bytes 13832 | tf_op jit(solution)/shard_map/ppermute | solution.py:19
  6.2 5.0 %collective-permute-start.5 = (f32[3,3,128]{2,1,0:T(4,128)S(1)}, f32[3,3,128]{2,1,0:T(4,128)S(1)}, u32[]{:S(2)}, u32[]{:S(2)}) collective-permute-start(f32[3,3,128]{2,1,0:T(4,128)S(1)} %get-tuple-element.543), channel_id=1, source_target_pairs={{16,0},{32,16},{48,32},{64,48},{80,64},{96,80},{112,96},{128,112},... | collective-permute-start | bytes 13832 | tf_op jit(solution)/shard_map/ppermute | solution.py:22
  12.1 5.6 %collective-permute-start.7 = (f32[3,38,3]{2,1,0:T(8,128)S(1)}, f32[3,38,3]{2,1,0:T(8,128)S(1)}, u32[]{:S(2)}, u32[]{:S(2)}) collective-permute-start(f32[3,38,3]{2,1,0:T(8,128)S(1)} %get-tuple-element.538), channel_id=1, source_target_pairs={{0,1},{1,2},{2,3},{3,4},{4,5},{5,6},{6,7},{7,8},{8,9},{9,10},{10,1... | collective-permute-start | bytes 4112 | tf_op jit(solution)/shard_map/ppermute | solution.py:19
  19.7 4.5 %collective-permute-done.6 = f32[3,38,3]{2,1,0:T(8,128)S(1)} collective-permute-done((f32[3,38,3]{2,1,0:T(8,128)S(1)}, f32[3,38,3]{2,1,0:T(8,128)S(1)}, u32[]{:S(2)}, u32[]{:S(2)}) %collective-permute-start.6) | collective-permute-done | bytes 1400 | tf_op jit(solution)/shard_map/ppermute | solution.py:22
  26.8 218.6 %while.19 = (s32[]{:T(128)}, f32[2,32,128]{2,1,0:T(8,128)S(1)}, f32[2,32,128]{2,1,0:T(8,128)S(1)}, f32[2,32,128]{2,1,0:T(8,128)S(1)}, s32[2,32,128]{2,1,0:T(8,12...) while((s32[]{:T(128)}, f32[2,32,128]{2,1,0:T(8,128)S(1)}, ...), condition=%wide.region_1.2_spmd, body=%wide.region_0.1_spmd.sunk | while | flops 4905138 | bytes 3933845 | solution.py:87
  26.9 5.6 %collective-permute-start = (f32[3,3,128]{2,1,0:T(4,128)S(1)}, f32[3,3,128]{2,1,0:T(4,128)S(1)}, u32[]{:S(2)}, u32[]{:S(2)}) collective-permute-start(f32[3,3,128]{2,1,0:T(4,128)S(1)} %get-tuple-element.662), channel_id=1, source_target_pairs={{16,0},{32,16},{48,32},{64,48},{80,64},{96,80},{112,96},{128,112},... | collective-permute-start | bytes 13832 | tf_op jit(solution)/shard_map/while/body/eval_jaxpr/ppermute | solution.py:22
  34.4 6.0 %collective-permute-done.1 = f32[3,3,128]{2,1,0:T(4,128)S(1)} collective-permute-done((f32[3,3,128]{2,1,0:T(4,128)S(1)}, f32[3,3,128]{2,1,0:T(4,128)S(1)}, u32[]{:S(2)}, u32[]{:S(2)}) %collective-permute-start.1) | collective-permute-done | bytes 4640 | tf_op jit(solution)/shard_map/while/body/eval_jaxpr/ppermute | solution.py:19
  40.6 3.9 %collective-permute-start.2 = (f32[3,38,3]{2,1,0:T(8,128)S(1)}, f32[3,38,3]{2,1,0:T(8,128)S(1)}, u32[]{:S(2)}, u32[]{:S(2)}) collective-permute-start(f32[3,38,3]{2,1,0:T(8,128)S(1)} %get-tuple-element.664), channel_id=1, source_target_pairs={{0,1},{1,2},{2,3},{3,4},{4,5},{5,6},{6,7},{7,8},{8,9},{9,10},{10,1... | collective-permute-start | bytes 4112 | tf_op jit(solution)/shard_map/while/body/eval_jaxpr/ppermute | solution.py:19
  46.4 4.5 %collective-permute-done.3 = f32[3,38,3]{2,1,0:T(8,128)S(1)} collective-permute-done((f32[3,38,3]{2,1,0:T(8,128)S(1)}, f32[3,38,3]{2,1,0:T(8,128)S(1)}, u32[]{:S(2)}, u32[]{:S(2)}) %collective-permute-start.3) | collective-permute-done | bytes 1400 | tf_op jit(solution)/shard_map/while/body/eval_jaxpr/ppermute | solution.py:22
  54.2 4.9 %collective-permute-start.1 = (f32[3,3,128]{2,1,0:T(4,128)S(1)}, f32[3,3,128]{2,1,0:T(4,128)S(1)}, u32[]{:S(2)}, u32[]{:S(2)}) collective-permute-start(f32[3,3,128]{2,1,0:T(4,128)S(1)} %get-tuple-element.663), channel_id=1, source_target_pairs={{0,16},{16,32},{32,48},{48,64},{64,80},{80,96},{96,112},{112,128},... | collective-permute-start | bytes 13832 | tf_op jit(solution)/shard_map/while/body/eval_jaxpr/ppermute | solution.py:19
  67.3 4.5 %collective-permute-done.3 = f32[3,38,3]{2,1,0:T(8,128)S(1)} collective-permute-done((f32[3,38,3]{2,1,0:T(8,128)S(1)}, f32[3,38,3]{2,1,0:T(8,128)S(1)}, u32[]{:S(2)}, u32[]{:S(2)}) %collective-permute-start.3) | collective-permute-done | bytes 1400 | tf_op jit(solution)/shard_map/while/body/eval_jaxpr/ppermute | solution.py:22
  75.1 4.9 %collective-permute-start.1 = (f32[3,3,128]{2,1,0:T(4,128)S(1)}, f32[3,3,128]{2,1,0:T(4,128)S(1)}, u32[]{:S(2)}, u32[]{:S(2)}) collective-permute-start(f32[3,3,128]{2,1,0:T(4,128)S(1)} %get-tuple-element.663), channel_id=1, source_target_pairs={{0,16},{16,32},{32,48},{48,64},{64,80},{80,96},{96,112},{112,128},... | collective-permute-start | bytes 13832 | tf_op jit(solution)/shard_map/while/body/eval_jaxpr/ppermute | solution.py:19
  88.2 4.5 %collective-permute-done.3 = f32[3,38,3]{2,1,0:T(8,128)S(1)} collective-permute-done((f32[3,38,3]{2,1,0:T(8,128)S(1)}, f32[3,38,3]{2,1,0:T(8,128)S(1)}, u32[]{:S(2)}, u32[]{:S(2)}) %collective-permute-start.3) | collective-permute-done | bytes 1400 | tf_op jit(solution)/shard_map/while/body/eval_jaxpr/ppermute | solution.py:22
  96.0 4.9 %collective-permute-start.1 = (f32[3,3,128]{2,1,0:T(4,128)S(1)}, f32[3,3,128]{2,1,0:T(4,128)S(1)}, u32[]{:S(2)}, u32[]{:S(2)}) collective-permute-start(f32[3,3,128]{2,1,0:T(4,128)S(1)} %get-tuple-element.663), channel_id=1, source_target_pairs={{0,16},{16,32},{32,48},{48,64},{64,80},{80,96},{96,112},{112,128},... | collective-permute-start | bytes 13832 | tf_op jit(solution)/shard_map/while/body/eval_jaxpr/ppermute | solution.py:19
  109.1 4.5 %collective-permute-done.3 = f32[3,38,3]{2,1,0:T(8,128)S(1)} collective-permute-done((f32[3,38,3]{2,1,0:T(8,128)S(1)}, f32[3,38,3]{2,1,0:T(8,128)S(1)}, u32[]{:S(2)}, u32[]{:S(2)}) %collective-permute-start.3) | collective-permute-done | bytes 1400 | tf_op jit(solution)/shard_map/while/body/eval_jaxpr/ppermute | solution.py:22
  116.9 4.9 %collective-permute-start.1 = (f32[3,3,128]{2,1,0:T(4,128)S(1)}, f32[3,3,128]{2,1,0:T(4,128)S(1)}, u32[]{:S(2)}, u32[]{:S(2)}) collective-permute-start(f32[3,3,128]{2,1,0:T(4,128)S(1)} %get-tuple-element.663), channel_id=1, source_target_pairs={{0,16},{16,32},{32,48},{48,64},{64,80},{80,96},{96,112},{112,128},... | collective-permute-start | bytes 13832 | tf_op jit(solution)/shard_map/while/body/eval_jaxpr/ppermute | solution.py:19
  130.0 4.5 %collective-permute-done.3 = f32[3,38,3]{2,1,0:T(8,128)S(1)} collective-permute-done((f32[3,38,3]{2,1,0:T(8,128)S(1)}, f32[3,38,3]{2,1,0:T(8,128)S(1)}, u32[]{:S(2)}, u32[]{:S(2)}) %collective-permute-start.3) | collective-permute-done | bytes 1400 | tf_op jit(solution)/shard_map/while/body/eval_jaxpr/ppermute | solution.py:22
  137.9 4.9 %collective-permute-start.1 = (f32[3,3,128]{2,1,0:T(4,128)S(1)}, f32[3,3,128]{2,1,0:T(4,128)S(1)}, u32[]{:S(2)}, u32[]{:S(2)}) collective-permute-start(f32[3,3,128]{2,1,0:T(4,128)S(1)} %get-tuple-element.663), channel_id=1, source_target_pairs={{0,16},{16,32},{32,48},{48,64},{64,80},{80,96},{96,112},{112,128},... | collective-permute-start | bytes 13832 | tf_op jit(solution)/shard_map/while/body/eval_jaxpr/ppermute | solution.py:19
  150.9 4.5 %collective-permute-done.3 = f32[3,38,3]{2,1,0:T(8,128)S(1)} collective-permute-done((f32[3,38,3]{2,1,0:T(8,128)S(1)}, f32[3,38,3]{2,1,0:T(8,128)S(1)}, u32[]{:S(2)}, u32[]{:S(2)}) %collective-permute-start.3) | collective-permute-done | bytes 1400 | tf_op jit(solution)/shard_map/while/body/eval_jaxpr/ppermute | solution.py:22
  158.8 4.9 %collective-permute-start.1 = (f32[3,3,128]{2,1,0:T(4,128)S(1)}, f32[3,3,128]{2,1,0:T(4,128)S(1)}, u32[]{:S(2)}, u32[]{:S(2)}) collective-permute-start(f32[3,3,128]{2,1,0:T(4,128)S(1)} %get-tuple-element.663), channel_id=1, source_target_pairs={{0,16},{16,32},{32,48},{48,64},{64,80},{80,96},{96,112},{112,128},... | collective-permute-start | bytes 13832 | tf_op jit(solution)/shard_map/while/body/eval_jaxpr/ppermute | solution.py:19
  166.8 3.7 %collective-permute-start.2 = (f32[3,38,3]{2,1,0:T(8,128)S(1)}, f32[3,38,3]{2,1,0:T(8,128)S(1)}, u32[]{:S(2)}, u32[]{:S(2)}) collective-permute-start(f32[3,38,3]{2,1,0:T(8,128)S(1)} %get-tuple-element.664), channel_id=1, source_target_pairs={{0,1},{1,2},{2,3},{3,4},{4,5},{5,6},{6,7},{7,8},{8,9},{9,10},{10,1... | collective-permute-start | bytes 4112 | tf_op jit(solution)/shard_map/while/body/eval_jaxpr/ppermute | solution.py:19
  172.5 4.5 %collective-permute-done.3 = f32[3,38,3]{2,1,0:T(8,128)S(1)} collective-permute-done((f32[3,38,3]{2,1,0:T(8,128)S(1)}, f32[3,38,3]{2,1,0:T(8,128)S(1)}, u32[]{:S(2)}, u32[]{:S(2)}) %collective-permute-start.3) | collective-permute-done | bytes 1400 | tf_op jit(solution)/shard_map/while/body/eval_jaxpr/ppermute | solution.py:22
  181.4 3.8 %collective-permute-start.1 = (f32[3,3,128]{2,1,0:T(4,128)S(1)}, f32[3,3,128]{2,1,0:T(4,128)S(1)}, u32[]{:S(2)}, u32[]{:S(2)}) collective-permute-start(f32[3,3,128]{2,1,0:T(4,128)S(1)} %get-tuple-element.663), channel_id=1, source_target_pairs={{0,16},{16,32},{32,48},{48,64},{64,80},{80,96},{96,112},{112,128},... | collective-permute-start | bytes 13832 | tf_op jit(solution)/shard_map/while/body/eval_jaxpr/ppermute | solution.py:19
  185.2 4.2 %collective-permute-done.1 = f32[3,3,128]{2,1,0:T(4,128)S(1)} collective-permute-done((f32[3,3,128]{2,1,0:T(4,128)S(1)}, f32[3,3,128]{2,1,0:T(4,128)S(1)}, u32[]{:S(2)}, u32[]{:S(2)}) %collective-permute-start.1) | collective-permute-done | bytes 4640 | tf_op jit(solution)/shard_map/while/body/eval_jaxpr/ppermute | solution.py:19
  189.5 3.9 %collective-permute-start.2 = (f32[3,38,3]{2,1,0:T(8,128)S(1)}, f32[3,38,3]{2,1,0:T(8,128)S(1)}, u32[]{:S(2)}, u32[]{:S(2)}) collective-permute-start(f32[3,38,3]{2,1,0:T(8,128)S(1)} %get-tuple-element.664), channel_id=1, source_target_pairs={{0,1},{1,2},{2,3},{3,4},{4,5},{5,6},{6,7},{7,8},{8,9},{9,10},{10,1... | collective-permute-start | bytes 4112 | tf_op jit(solution)/shard_map/while/body/eval_jaxpr/ppermute | solution.py:19
  195.3 4.5 %collective-permute-done.3 = f32[3,38,3]{2,1,0:T(8,128)S(1)} collective-permute-done((f32[3,38,3]{2,1,0:T(8,128)S(1)}, f32[3,38,3]{2,1,0:T(8,128)S(1)}, u32[]{:S(2)}, u32[]{:S(2)}) %collective-permute-start.3) | collective-permute-done | bytes 1400 | tf_op jit(solution)/shard_map/while/body/eval_jaxpr/ppermute | solution.py:22
  201.2 3.4 %collective-permute-start = (f32[3,3,128]{2,1,0:T(4,128)S(1)}, f32[3,3,128]{2,1,0:T(4,128)S(1)}, u32[]{:S(2)}, u32[]{:S(2)}) collective-permute-start(f32[3,3,128]{2,1,0:T(4,128)S(1)} %get-tuple-element.662), channel_id=1, source_target_pairs={{16,0},{32,16},{48,32},{64,48},{80,64},{96,80},{112,96},{128,112},... | collective-permute-start | bytes 13832 | tf_op jit(solution)/shard_map/while/body/eval_jaxpr/ppermute | solution.py:22
  208.1 4.6 %collective-permute-done.1 = f32[3,3,128]{2,1,0:T(4,128)S(1)} collective-permute-done((f32[3,3,128]{2,1,0:T(4,128)S(1)}, f32[3,3,128]{2,1,0:T(4,128)S(1)}, u32[]{:S(2)}, u32[]{:S(2)}) %collective-permute-start.1) | collective-permute-done | bytes 4640 | tf_op jit(solution)/shard_map/while/body/eval_jaxpr/ppermute | solution.py:19
  212.8 3.9 %collective-permute-start.2 = (f32[3,38,3]{2,1,0:T(8,128)S(1)}, f32[3,38,3]{2,1,0:T(8,128)S(1)}, u32[]{:S(2)}, u32[]{:S(2)}) collective-permute-start(f32[3,38,3]{2,1,0:T(8,128)S(1)} %get-tuple-element.664), channel_id=1, source_target_pairs={{0,1},{1,2},{2,3},{3,4},{4,5},{5,6},{6,7},{7,8},{8,9},{9,10},{10,1... | collective-permute-start | bytes 4112 | tf_op jit(solution)/shard_map/while/body/eval_jaxpr/ppermute | solution.py:19
  218.6 4.5 %collective-permute-done.3 = f32[3,38,3]{2,1,0:T(8,128)S(1)} collective-permute-done((f32[3,38,3]{2,1,0:T(8,128)S(1)}, f32[3,38,3]{2,1,0:T(8,128)S(1)}, u32[]{:S(2)}, u32[]{:S(2)}) %collective-permute-start.3) | collective-permute-done | bytes 1400 | tf_op jit(solution)/shard_map/while/body/eval_jaxpr/ppermute | solution.py:22
  226.4 4.9 %collective-permute-start.1 = (f32[3,3,128]{2,1,0:T(4,128)S(1)}, f32[3,3,128]{2,1,0:T(4,128)S(1)}, u32[]{:S(2)}, u32[]{:S(2)}) collective-permute-start(f32[3,3,128]{2,1,0:T(4,128)S(1)} %get-tuple-element.663), channel_id=1, source_target_pairs={{0,16},{16,32},{32,48},{48,64},{64,80},{80,96},{96,112},{112,128},... | collective-permute-start | bytes 13832 | tf_op jit(solution)/shard_map/while/body/eval_jaxpr/ppermute | solution.py:19
  239.6 4.5 %collective-permute-done.3 = f32[3,38,3]{2,1,0:T(8,128)S(1)} collective-permute-done((f32[3,38,3]{2,1,0:T(8,128)S(1)}, f32[3,38,3]{2,1,0:T(8,128)S(1)}, u32[]{:S(2)}, u32[]{:S(2)}) %collective-permute-start.3) | collective-permute-done | bytes 1400 | tf_op jit(solution)/shard_map/while/body/eval_jaxpr/ppermute | solution.py:22
  (180 shorter events, 103.2 us)
Async XLA Ops:
  2.1 9.1 %collective-permute-start.4 = (f32[3,3,128]{2,1,0:T(4,128)S(1)}, f32[3,3,128]{2,1,0:T(4,128)S(1)}, u32[]{:S(2)}, u32[]{:S(2)}) collective-permute-start(f32[3,3,128]{2,1,0:T(4,128)S(1)} %get-tuple-element.542), channel_id=1, source_target_pairs={{0,16},{16,32},{32,48},{48,64},{64,80},{80,96},{96,112},{112,128},... | collective-permute-start | bytes 13832 | tf_op jit(solution)/shard_map/ppermute | solution.py:19
  12.1 7.6 %collective-permute-start.7 = (f32[3,38,3]{2,1,0:T(8,128)S(1)}, f32[3,38,3]{2,1,0:T(8,128)S(1)}, u32[]{:S(2)}, u32[]{:S(2)}) collective-permute-start(f32[3,38,3]{2,1,0:T(8,128)S(1)} %get-tuple-element.538), channel_id=1, source_target_pairs={{0,1},{1,2},{2,3},{3,4},{4,5},{5,6},{6,7},{7,8},{8,9},{9,10},{10,1... | collective-permute-start | bytes 4112 | tf_op jit(solution)/shard_map/ppermute | solution.py:19
  17.7 6.4 %collective-permute-start.6 = (f32[3,38,3]{2,1,0:T(8,128)S(1)}, f32[3,38,3]{2,1,0:T(8,128)S(1)}, u32[]{:S(2)}, u32[]{:S(2)}) collective-permute-start(f32[3,38,3]{2,1,0:T(8,128)S(1)} %get-tuple-element.539), channel_id=1, source_target_pairs={{1,0},{2,1},{3,2},{4,3},{5,4},{6,5},{7,6},{8,7},{9,8},{10,9},{11,1... | collective-permute-start | bytes 4112 | tf_op jit(solution)/shard_map/ppermute | solution.py:22
  26.9 7.5 %collective-permute-start = (f32[3,3,128]{2,1,0:T(4,128)S(1)}, f32[3,3,128]{2,1,0:T(4,128)S(1)}, u32[]{:S(2)}, u32[]{:S(2)}) collective-permute-start(f32[3,3,128]{2,1,0:T(4,128)S(1)} %get-tuple-element.662), channel_id=1, source_target_pairs={{16,0},{32,16},{48,32},{64,48},{80,64},{96,80},{112,96},{128,112},... | collective-permute-start | bytes 13832 | tf_op jit(solution)/shard_map/while/body/eval_jaxpr/ppermute | solution.py:22
  32.5 8.0 %collective-permute-start.1 = (f32[3,3,128]{2,1,0:T(4,128)S(1)}, f32[3,3,128]{2,1,0:T(4,128)S(1)}, u32[]{:S(2)}, u32[]{:S(2)}) collective-permute-start(f32[3,3,128]{2,1,0:T(4,128)S(1)} %get-tuple-element.663), channel_id=1, source_target_pairs={{0,16},{16,32},{32,48},{48,64},{64,80},{80,96},{96,112},{112,128},... | collective-permute-start | bytes 13832 | tf_op jit(solution)/shard_map/while/body/eval_jaxpr/ppermute | solution.py:19
  44.5 6.4 %collective-permute-start.3 = (f32[3,38,3]{2,1,0:T(8,128)S(1)}, f32[3,38,3]{2,1,0:T(8,128)S(1)}, u32[]{:S(2)}, u32[]{:S(2)}) collective-permute-start(f32[3,38,3]{2,1,0:T(8,128)S(1)} %get-tuple-element.665), channel_id=1, source_target_pairs={{1,0},{2,1},{3,2},{4,3},{5,4},{6,5},{7,6},{8,7},{9,8},{10,9},{11,1... | collective-permute-start | bytes 4112 | tf_op jit(solution)/shard_map/while/body/eval_jaxpr/ppermute | solution.py:22
  52.3 6.8 %collective-permute-start = (f32[3,3,128]{2,1,0:T(4,128)S(1)}, f32[3,3,128]{2,1,0:T(4,128)S(1)}, u32[]{:S(2)}, u32[]{:S(2)}) collective-permute-start(f32[3,3,128]{2,1,0:T(4,128)S(1)} %get-tuple-element.662), channel_id=1, source_target_pairs={{16,0},{32,16},{48,32},{64,48},{80,64},{96,80},{112,96},{128,112},... | collective-permute-start | bytes 13832 | tf_op jit(solution)/shard_map/while/body/eval_jaxpr/ppermute | solution.py:22
  54.2 8.0 %collective-permute-start.1 = (f32[3,3,128]{2,1,0:T(4,128)S(1)}, f32[3,3,128]{2,1,0:T(4,128)S(1)}, u32[]{:S(2)}, u32[]{:S(2)}) collective-permute-start(f32[3,3,128]{2,1,0:T(4,128)S(1)} %get-tuple-element.663), channel_id=1, source_target_pairs={{0,16},{16,32},{32,48},{48,64},{64,80},{80,96},{96,112},{112,128},... | collective-permute-start | bytes 13832 | tf_op jit(solution)/shard_map/while/body/eval_jaxpr/ppermute | solution.py:19
  65.4 6.4 %collective-permute-start.3 = (f32[3,38,3]{2,1,0:T(8,128)S(1)}, f32[3,38,3]{2,1,0:T(8,128)S(1)}, u32[]{:S(2)}, u32[]{:S(2)}) collective-permute-start(f32[3,38,3]{2,1,0:T(8,128)S(1)} %get-tuple-element.665), channel_id=1, source_target_pairs={{1,0},{2,1},{3,2},{4,3},{5,4},{6,5},{7,6},{8,7},{9,8},{10,9},{11,1... | collective-permute-start | bytes 4112 | tf_op jit(solution)/shard_map/while/body/eval_jaxpr/ppermute | solution.py:22
  73.2 6.8 %collective-permute-start = (f32[3,3,128]{2,1,0:T(4,128)S(1)}, f32[3,3,128]{2,1,0:T(4,128)S(1)}, u32[]{:S(2)}, u32[]{:S(2)}) collective-permute-start(f32[3,3,128]{2,1,0:T(4,128)S(1)} %get-tuple-element.662), channel_id=1, source_target_pairs={{16,0},{32,16},{48,32},{64,48},{80,64},{96,80},{112,96},{128,112},... | collective-permute-start | bytes 13832 | tf_op jit(solution)/shard_map/while/body/eval_jaxpr/ppermute | solution.py:22
  75.1 8.0 %collective-permute-start.1 = (f32[3,3,128]{2,1,0:T(4,128)S(1)}, f32[3,3,128]{2,1,0:T(4,128)S(1)}, u32[]{:S(2)}, u32[]{:S(2)}) collective-permute-start(f32[3,3,128]{2,1,0:T(4,128)S(1)} %get-tuple-element.663), channel_id=1, source_target_pairs={{0,16},{16,32},{32,48},{48,64},{64,80},{80,96},{96,112},{112,128},... | collective-permute-start | bytes 13832 | tf_op jit(solution)/shard_map/while/body/eval_jaxpr/ppermute | solution.py:19
  86.2 6.4 %collective-permute-start.3 = (f32[3,38,3]{2,1,0:T(8,128)S(1)}, f32[3,38,3]{2,1,0:T(8,128)S(1)}, u32[]{:S(2)}, u32[]{:S(2)}) collective-permute-start(f32[3,38,3]{2,1,0:T(8,128)S(1)} %get-tuple-element.665), channel_id=1, source_target_pairs={{1,0},{2,1},{3,2},{4,3},{5,4},{6,5},{7,6},{8,7},{9,8},{10,9},{11,1... | collective-permute-start | bytes 4112 | tf_op jit(solution)/shard_map/while/body/eval_jaxpr/ppermute | solution.py:22
  94.1 6.8 %collective-permute-start = (f32[3,3,128]{2,1,0:T(4,128)S(1)}, f32[3,3,128]{2,1,0:T(4,128)S(1)}, u32[]{:S(2)}, u32[]{:S(2)}) collective-permute-start(f32[3,3,128]{2,1,0:T(4,128)S(1)} %get-tuple-element.662), channel_id=1, source_target_pairs={{16,0},{32,16},{48,32},{64,48},{80,64},{96,80},{112,96},{128,112},... | collective-permute-start | bytes 13832 | tf_op jit(solution)/shard_map/while/body/eval_jaxpr/ppermute | solution.py:22
  96.0 8.0 %collective-permute-start.1 = (f32[3,3,128]{2,1,0:T(4,128)S(1)}, f32[3,3,128]{2,1,0:T(4,128)S(1)}, u32[]{:S(2)}, u32[]{:S(2)}) collective-permute-start(f32[3,3,128]{2,1,0:T(4,128)S(1)} %get-tuple-element.663), channel_id=1, source_target_pairs={{0,16},{16,32},{32,48},{48,64},{64,80},{80,96},{96,112},{112,128},... | collective-permute-start | bytes 13832 | tf_op jit(solution)/shard_map/while/body/eval_jaxpr/ppermute | solution.py:19
  107.1 6.4 %collective-permute-start.3 = (f32[3,38,3]{2,1,0:T(8,128)S(1)}, f32[3,38,3]{2,1,0:T(8,128)S(1)}, u32[]{:S(2)}, u32[]{:S(2)}) collective-permute-start(f32[3,38,3]{2,1,0:T(8,128)S(1)} %get-tuple-element.665), channel_id=1, source_target_pairs={{1,0},{2,1},{3,2},{4,3},{5,4},{6,5},{7,6},{8,7},{9,8},{10,9},{11,1... | collective-permute-start | bytes 4112 | tf_op jit(solution)/shard_map/while/body/eval_jaxpr/ppermute | solution.py:22
  115.0 6.8 %collective-permute-start = (f32[3,3,128]{2,1,0:T(4,128)S(1)}, f32[3,3,128]{2,1,0:T(4,128)S(1)}, u32[]{:S(2)}, u32[]{:S(2)}) collective-permute-start(f32[3,3,128]{2,1,0:T(4,128)S(1)} %get-tuple-element.662), channel_id=1, source_target_pairs={{16,0},{32,16},{48,32},{64,48},{80,64},{96,80},{112,96},{128,112},... | collective-permute-start | bytes 13832 | tf_op jit(solution)/shard_map/while/body/eval_jaxpr/ppermute | solution.py:22
  116.9 8.0 %collective-permute-start.1 = (f32[3,3,128]{2,1,0:T(4,128)S(1)}, f32[3,3,128]{2,1,0:T(4,128)S(1)}, u32[]{:S(2)}, u32[]{:S(2)}) collective-permute-start(f32[3,3,128]{2,1,0:T(4,128)S(1)} %get-tuple-element.663), channel_id=1, source_target_pairs={{0,16},{16,32},{32,48},{48,64},{64,80},{80,96},{96,112},{112,128},... | collective-permute-start | bytes 13832 | tf_op jit(solution)/shard_map/while/body/eval_jaxpr/ppermute | solution.py:19
  128.1 6.4 %collective-permute-start.3 = (f32[3,38,3]{2,1,0:T(8,128)S(1)}, f32[3,38,3]{2,1,0:T(8,128)S(1)}, u32[]{:S(2)}, u32[]{:S(2)}) collective-permute-start(f32[3,38,3]{2,1,0:T(8,128)S(1)} %get-tuple-element.665), channel_id=1, source_target_pairs={{1,0},{2,1},{3,2},{4,3},{5,4},{6,5},{7,6},{8,7},{9,8},{10,9},{11,1... | collective-permute-start | bytes 4112 | tf_op jit(solution)/shard_map/while/body/eval_jaxpr/ppermute | solution.py:22
  135.9 6.8 %collective-permute-start = (f32[3,3,128]{2,1,0:T(4,128)S(1)}, f32[3,3,128]{2,1,0:T(4,128)S(1)}, u32[]{:S(2)}, u32[]{:S(2)}) collective-permute-start(f32[3,3,128]{2,1,0:T(4,128)S(1)} %get-tuple-element.662), channel_id=1, source_target_pairs={{16,0},{32,16},{48,32},{64,48},{80,64},{96,80},{112,96},{128,112},... | collective-permute-start | bytes 13832 | tf_op jit(solution)/shard_map/while/body/eval_jaxpr/ppermute | solution.py:22
  137.9 8.0 %collective-permute-start.1 = (f32[3,3,128]{2,1,0:T(4,128)S(1)}, f32[3,3,128]{2,1,0:T(4,128)S(1)}, u32[]{:S(2)}, u32[]{:S(2)}) collective-permute-start(f32[3,3,128]{2,1,0:T(4,128)S(1)} %get-tuple-element.663), channel_id=1, source_target_pairs={{0,16},{16,32},{32,48},{48,64},{64,80},{80,96},{96,112},{112,128},... | collective-permute-start | bytes 13832 | tf_op jit(solution)/shard_map/while/body/eval_jaxpr/ppermute | solution.py:19
  149.0 6.4 %collective-permute-start.3 = (f32[3,38,3]{2,1,0:T(8,128)S(1)}, f32[3,38,3]{2,1,0:T(8,128)S(1)}, u32[]{:S(2)}, u32[]{:S(2)}) collective-permute-start(f32[3,38,3]{2,1,0:T(8,128)S(1)} %get-tuple-element.665), channel_id=1, source_target_pairs={{1,0},{2,1},{3,2},{4,3},{5,4},{6,5},{7,6},{8,7},{9,8},{10,9},{11,1... | collective-permute-start | bytes 4112 | tf_op jit(solution)/shard_map/while/body/eval_jaxpr/ppermute | solution.py:22
  156.8 6.8 %collective-permute-start = (f32[3,3,128]{2,1,0:T(4,128)S(1)}, f32[3,3,128]{2,1,0:T(4,128)S(1)}, u32[]{:S(2)}, u32[]{:S(2)}) collective-permute-start(f32[3,3,128]{2,1,0:T(4,128)S(1)} %get-tuple-element.662), channel_id=1, source_target_pairs={{16,0},{32,16},{48,32},{64,48},{80,64},{96,80},{112,96},{128,112},... | collective-permute-start | bytes 13832 | tf_op jit(solution)/shard_map/while/body/eval_jaxpr/ppermute | solution.py:22
  158.8 8.0 %collective-permute-start.1 = (f32[3,3,128]{2,1,0:T(4,128)S(1)}, f32[3,3,128]{2,1,0:T(4,128)S(1)}, u32[]{:S(2)}, u32[]{:S(2)}) collective-permute-start(f32[3,3,128]{2,1,0:T(4,128)S(1)} %get-tuple-element.663), channel_id=1, source_target_pairs={{0,16},{16,32},{32,48},{48,64},{64,80},{80,96},{96,112},{112,128},... | collective-permute-start | bytes 13832 | tf_op jit(solution)/shard_map/while/body/eval_jaxpr/ppermute | solution.py:19
  170.5 6.4 %collective-permute-start.3 = (f32[3,38,3]{2,1,0:T(8,128)S(1)}, f32[3,38,3]{2,1,0:T(8,128)S(1)}, u32[]{:S(2)}, u32[]{:S(2)}) collective-permute-start(f32[3,38,3]{2,1,0:T(8,128)S(1)} %get-tuple-element.665), channel_id=1, source_target_pairs={{1,0},{2,1},{3,2},{4,3},{5,4},{6,5},{7,6},{8,7},{9,8},{10,9},{11,1... | collective-permute-start | bytes 4112 | tf_op jit(solution)/shard_map/while/body/eval_jaxpr/ppermute | solution.py:22
  178.4 6.8 %collective-permute-start = (f32[3,3,128]{2,1,0:T(4,128)S(1)}, f32[3,3,128]{2,1,0:T(4,128)S(1)}, u32[]{:S(2)}, u32[]{:S(2)}) collective-permute-start(f32[3,3,128]{2,1,0:T(4,128)S(1)} %get-tuple-element.662), channel_id=1, source_target_pairs={{16,0},{32,16},{48,32},{64,48},{80,64},{96,80},{112,96},{128,112},... | collective-permute-start | bytes 13832 | tf_op jit(solution)/shard_map/while/body/eval_jaxpr/ppermute | solution.py:22
  181.4 8.0 %collective-permute-start.1 = (f32[3,3,128]{2,1,0:T(4,128)S(1)}, f32[3,3,128]{2,1,0:T(4,128)S(1)}, u32[]{:S(2)}, u32[]{:S(2)}) collective-permute-start(f32[3,3,128]{2,1,0:T(4,128)S(1)} %get-tuple-element.663), channel_id=1, source_target_pairs={{0,16},{16,32},{32,48},{48,64},{64,80},{80,96},{96,112},{112,128},... | collective-permute-start | bytes 13832 | tf_op jit(solution)/shard_map/while/body/eval_jaxpr/ppermute | solution.py:19
  193.4 6.4 %collective-permute-start.3 = (f32[3,38,3]{2,1,0:T(8,128)S(1)}, f32[3,38,3]{2,1,0:T(8,128)S(1)}, u32[]{:S(2)}, u32[]{:S(2)}) collective-permute-start(f32[3,38,3]{2,1,0:T(8,128)S(1)} %get-tuple-element.665), channel_id=1, source_target_pairs={{1,0},{2,1},{3,2},{4,3},{5,4},{6,5},{7,6},{8,7},{9,8},{10,9},{11,1... | collective-permute-start | bytes 4112 | tf_op jit(solution)/shard_map/while/body/eval_jaxpr/ppermute | solution.py:22
  201.2 6.8 %collective-permute-start = (f32[3,3,128]{2,1,0:T(4,128)S(1)}, f32[3,3,128]{2,1,0:T(4,128)S(1)}, u32[]{:S(2)}, u32[]{:S(2)}) collective-permute-start(f32[3,3,128]{2,1,0:T(4,128)S(1)} %get-tuple-element.662), channel_id=1, source_target_pairs={{16,0},{32,16},{48,32},{64,48},{80,64},{96,80},{112,96},{128,112},... | collective-permute-start | bytes 13832 | tf_op jit(solution)/shard_map/while/body/eval_jaxpr/ppermute | solution.py:22
  204.7 8.0 %collective-permute-start.1 = (f32[3,3,128]{2,1,0:T(4,128)S(1)}, f32[3,3,128]{2,1,0:T(4,128)S(1)}, u32[]{:S(2)}, u32[]{:S(2)}) collective-permute-start(f32[3,3,128]{2,1,0:T(4,128)S(1)} %get-tuple-element.663), channel_id=1, source_target_pairs={{0,16},{16,32},{32,48},{48,64},{64,80},{80,96},{96,112},{112,128},... | collective-permute-start | bytes 13832 | tf_op jit(solution)/shard_map/while/body/eval_jaxpr/ppermute | solution.py:19
  216.7 6.4 %collective-permute-start.3 = (f32[3,38,3]{2,1,0:T(8,128)S(1)}, f32[3,38,3]{2,1,0:T(8,128)S(1)}, u32[]{:S(2)}, u32[]{:S(2)}) collective-permute-start(f32[3,38,3]{2,1,0:T(8,128)S(1)} %get-tuple-element.665), channel_id=1, source_target_pairs={{1,0},{2,1},{3,2},{4,3},{5,4},{6,5},{7,6},{8,7},{9,8},{10,9},{11,1... | collective-permute-start | bytes 4112 | tf_op jit(solution)/shard_map/while/body/eval_jaxpr/ppermute | solution.py:22
  224.5 6.8 %collective-permute-start = (f32[3,3,128]{2,1,0:T(4,128)S(1)}, f32[3,3,128]{2,1,0:T(4,128)S(1)}, u32[]{:S(2)}, u32[]{:S(2)}) collective-permute-start(f32[3,3,128]{2,1,0:T(4,128)S(1)} %get-tuple-element.662), channel_id=1, source_target_pairs={{16,0},{32,16},{48,32},{64,48},{80,64},{96,80},{112,96},{128,112},... | collective-permute-start | bytes 13832 | tf_op jit(solution)/shard_map/while/body/eval_jaxpr/ppermute | solution.py:22
  226.4 8.0 %collective-permute-start.1 = (f32[3,3,128]{2,1,0:T(4,128)S(1)}, f32[3,3,128]{2,1,0:T(4,128)S(1)}, u32[]{:S(2)}, u32[]{:S(2)}) collective-permute-start(f32[3,3,128]{2,1,0:T(4,128)S(1)} %get-tuple-element.663), channel_id=1, source_target_pairs={{0,16},{16,32},{32,48},{48,64},{64,80},{80,96},{96,112},{112,128},... | collective-permute-start | bytes 13832 | tf_op jit(solution)/shard_map/while/body/eval_jaxpr/ppermute | solution.py:19
  (18 other events, 78.1 us)
where the time goes:
time: 248 us; the launch traced here: 246 us
  starting transfers between devices  138 us (56%)
  waiting for transfers between devices  86.6 us (35%)
  other arithmetic  15.3 us (6%)
  local copies, waits for them, and re-layouts  4.27 us (2%)
    ppermute x22, starting transfers between devices, extended_2(): lax.ppermute(lax.slice_in_dim(block, block.shape[dim] - width, None, axis...  86.4 us
    ppermute x22, starting transfers between devices, extended_2(): lax.ppermute(lax.slice_in_dim(block, 0, width, axis=dim), axis, backward)  51.6 us
    ppermute x22, waiting for transfers between devices, extended_2(): lax.ppermute(lax.slice_in_dim(block, 0, width, axis=dim), axis, backward)  50.1 us
    ppermute x22, waiting for transfers between devices, extended_2(): lax.ppermute(lax.slice_in_dim(block, block.shape[dim] - width, None, axis...  36.4 us
    add x10, other arithmetic, full_forces(): force_x = force_x + term_x  10.2 us
  transfers between devices with their start and end apart: 44, of which 22 were waited for; matrix products, arithmetic and copies ran while one was open for 0% of the time, Pallas kernels for 0%

commit v1 on v0

v1 whole, which is shorter than its diff:
```python
import functools
import math

import jax
import jax.numpy as jnp
from jax import lax
from jax.experimental import pallas as pl
from jax.experimental.pallas import tpu as pltpu
from jax.sharding import PartitionSpec as P

STEPS = 10
TIME_STEP = 0.04
ROWS = 32
COLS = 128
BASE = 48
TALL = 128
SIDE = 96
TINY = 1.2e-38
MESH = pl.DeviceIdType.MESH


def upper_shell():
    upper = []
    for row_step in range(0, 4):
        for col_step in range(-3, 4):
            if row_step * row_step + col_step * col_step <= 9 and (row_step > 0 or col_step > 0):
                upper.append((row_step, col_step))
    return upper


def half_shell():
    bonds = []
    for index, (row_step, col_step) in enumerate(upper_shell()):
        if col_step >= 0:
            bonds.append((row_step, col_step, index, False))
        else:
            bonds.append((-row_step, -col_step, index, True))
    return sorted(bonds, key=lambda bond: (bond[1], bond[0]))


BONDS = half_shell()


def lanes_of(shape):
    return lax.broadcasted_iota(jnp.int32, shape, len(shape) - 1)


def ahead(first, second, step):
    if step == 0:
        return first, second
    inside = lanes_of(first.shape) < COLS - step
    a, b = pltpu.roll(first, COLS - step, 1), pltpu.roll(second, COLS - step, 1)
    return jnp.where(inside, a, b), jnp.where(inside, b, a)


def behind(first, second, step):
    if step == 0:
        return first, second
    inside = lanes_of(first.shape) >= step
    a, b = pltpu.roll(first, step, 1), pltpu.roll(second, step, 1)
    return jnp.where(inside, a, b), jnp.where(inside, b, a)


def packed(fields, starts, group_starts):
    lanes = lanes_of((ROWS, COLS))
    total = None
    for field, start, group in zip(fields, starts, group_starts, strict=True):
        moved = pltpu.roll(field, (group - start) % COLS, 1)
        total = moved if total is None else jnp.where((lanes >= group) & (lanes < group + 32), moved, total)
    return total


def exchange_kernel(shape_x, shape_y, disp, vel, stiff, body, bits, ext, left, right,
                    bits_own, to_west, to_east, local_sem, send_sem, recv_sem):
    gx, gy = lax.axis_index("gx"), lax.axis_index("gy")

    def neighbour(row_step, col_step):
        return (
            lax.rem(gx + row_step + shape_x, shape_x),
            lax.rem(gy + col_step + shape_y, shape_y),
        )

    around = [(-1, 0), (1, 0), (0, -1), (0, 1), (-1, -1), (-1, 1), (1, -1), (1, 1), (-2, 0), (2, 0)]
    barrier = pltpu.get_barrier_semaphore()
    for step in around:
        pl.semaphore_signal(barrier, inc=1, device_id=neighbour(*step), device_id_type=MESH)

    own = pl.ds(BASE, ROWS)
    local = [
        pltpu.make_async_copy(bits.at[0], bits_own, local_sem.at[0]),
        pltpu.make_async_copy(disp, ext.at[pl.ds(0, 2), own], local_sem.at[1]),
        pltpu.make_async_copy(stiff, ext.at[2, own], local_sem.at[2]),
        pltpu.make_async_copy(vel, ext.at[pl.ds(4, 2), own], local_sem.at[3]),
        pltpu.make_async_copy(body, ext.at[pl.ds(6, 2), own], local_sem.at[4]),
    ]
    for copy in local:
        copy.start()
    for copy in local:
        copy.wait()
    ext[3, own] = bits_own[...].astype(jnp.float32)

    near = [ext[field, own] for field in range(8)]
    lanes = lanes_of((ROWS, COLS))
    groups = [0, 32, 64, 96]
    to_west[0] = packed(near[:4], [0] * 4, groups)
    to_east[0] = packed(near[:4], [96] * 4, groups)
    west, east = packed(near[4:], [0] * 4, groups), packed(near[4:], [96] * 4, groups)
    for field in range(4):
        group = groups[field]
        west = jnp.where(lanes == group + 30, pltpu.roll(near[field], (group + 30 - 32) % COLS, 1), west)
        east = jnp.where(lanes == group + 1, pltpu.roll(near[field], (group + 1 - 95) % COLS, 1), east)
    to_west[1] = west
    to_east[1] = east

    pl.semaphore_wait(barrier, len(around))

    near_fields, late_fields = pl.ds(0, 4), pl.ds(4, 4)
    plan = [
        (ext.at[near_fields, own], ext.at[near_fields, pl.ds(BASE + ROWS, ROWS)], (-1, 0)),
        (ext.at[near_fields, own], ext.at[near_fields, pl.ds(BASE - ROWS, ROWS)], (1, 0)),
        (to_west, right.at[:, pl.ds(64, 32)], (-1, -1)),
        (to_east, left.at[:, pl.ds(64, 32)], (-1, 1)),
        (to_west, right.at[:, pl.ds(0, 32)], (1, -1)),
        (to_east, left.at[:, pl.ds(0, 32)], (1, 1)),
        (to_west, right.at[:, pl.ds(32, 32)], (0, -1)),
        (to_east, left.at[:, pl.ds(32, 32)], (0, 1)),
        (ext.at[near_fields, pl.ds(BASE, 8)], ext.at[near_fields, pl.ds(BASE + 64, 8)], (-2, 0)),
        (ext.at[near_fields, pl.ds(BASE + 24, 8)], ext.at[near_fields, pl.ds(BASE - 40, 8)], (2, 0)),
        (ext.at[late_fields, own], ext.at[late_fields, pl.ds(BASE + ROWS, ROWS)], (-1, 0)),
        (ext.at[late_fields, own], ext.at[late_fields, pl.ds(BASE - ROWS, ROWS)], (1, 0)),
    ]
    copies = [
        pltpu.make_async_remote_copy(
            src_ref=source,
            dst_ref=target,
            send_sem=send_sem.at[index],
            recv_sem=recv_sem.at[index],
            device_id=neighbour(*step),
            device_id_type=MESH,
        )
        for index, (source, target, step) in enumerate(plan)
    ]
    for copy in copies:
        copy.start()
    for copy in copies:
        copy.wait_recv()
    for copy in copies:
        copy.wait_send()


def exchange(shape_x, shape_y, *args):
    any_space = pl.BlockSpec(memory_space=pl.ANY)
    vmem = pl.BlockSpec(memory_space=pltpu.VMEM)
    return pl.pallas_call(
        functools.partial(exchange_kernel, shape_x, shape_y),
        out_shape=(
            pltpu.VMEM((8, TALL, COLS), jnp.float32),
            pltpu.VMEM((2, SIDE, COLS), jnp.float32),
            pltpu.VMEM((2, SIDE, COLS), jnp.float32),
        ),
        in_specs=[any_space] * 5,
        out_specs=(vmem, vmem, vmem),
        scratch_shapes=[
            pltpu.VMEM((ROWS, COLS), jnp.int32),
            pltpu.VMEM((2, ROWS, COLS), jnp.float32),
            pltpu.VMEM((2, ROWS, COLS), jnp.float32),
            pltpu.SemaphoreType.DMA((5,)),
            pltpu.SemaphoreType.DMA((12,)),
            pltpu.SemaphoreType.DMA((12,)),
        ],
        compiler_params=pltpu.CompilerParams(collective_id=0, has_side_effects=True),
        name="exchange",
    )(*args)


def steps_kernel(ext, left, right, disp_out, vel_out, pos, half, push, coef, pair, near_sum, stiff, flags):
    lanes8 = lanes_of((8, COLS))
    low = lanes8 < 64

    def beside(word, group, rows):
        from_right = pltpu.roll(right[word, rows], (-32 * group) % COLS, 1)
        from_left = pltpu.roll(left[word, rows], (96 - 32 * group) % COLS, 1)
        return from_right, from_left

    def store_moved(buffer, rows, x, y):
        for step in range(4):
            mx, my = ahead(x[0], x[1], step), ahead(y[0], y[1], step)
            for tile in range(2):
                pos[buffer, 0, step, tile, rows] = mx[tile]
                pos[buffer, 1, step, tile, rows] = my[tile] + float(step) if step else my[tile]

    def set_up(index, carry):
        rows = pl.ds(pl.multiple_of(8 * index, 8), 8)
        side = pl.ds(pl.multiple_of(8 * index - 16, 8), 8)
        others = []
        for field in range(4):
            from_right, from_left = beside(0, field, side)
            value = jnp.where(lanes8 < 32, from_right, jnp.where(lanes8 >= 96, from_left, 0.0))
            far_right = pltpu.roll(right[1, side], (32 - (32 * field + 30)) % COLS, 1)
            far_left = pltpu.roll(left[1, side], (95 - (32 * field + 1)) % COLS, 1)
            value = jnp.where(lanes8 == 32, far_right, jnp.where(lanes8 == 95, far_left, value))
            others.append(value)
        own = [ext[field, rows] for field in range(4)]
        store_moved(0, rows, (own[0], others[0]), (own[1], others[1]))
        for step in range(4):
            moved = ahead(own[2], others[2], step)
            stiff[step, 0, rows], stiff[step, 1, rows] = moved
        for step in range(3):
            moved = ahead(own[3].astype(jnp.int32), others[3].astype(jnp.int32), step)
            flags[step, 0, rows], flags[step, 1, rows] = moved
        for component in range(2):
            half[component, 0, rows] = ext[4 + component, rows]
            push[component, 0, rows] = TIME_STEP * ext[6 + component, rows]
            from_right, from_left = beside(1, component, side)
            half[component, 1, rows] = jnp.where(lanes8 < 30, from_right, jnp.where(lanes8 >= 98, from_left, 0.0))
            from_right, from_left = beside(1, 2 + component, side)
            push[component, 1, rows] = TIME_STEP * jnp.where(
                lanes8 < 30, from_right, jnp.where(lanes8 >= 98, from_left, 0.0)
            )
        return carry

    zeros = jnp.zeros((8, COLS), jnp.float32)
    no_flags = jnp.zeros((8, COLS), jnp.int32)
    for index in (0, 1, 14, 15):
        rows = pl.ds(8 * index, 8)
        inside = index in (1, 14)
        x, y, k = (ext[field, rows] if inside else zeros for field in range(3))
        f = ext[3, rows].astype(jnp.int32) if inside else no_flags
        store_moved(0, rows, (x, zeros), (y, zeros))
        if index in (0, 15):
            for buffer_step in range(4):
                for tile in range(2):
                    pos[1, 0, buffer_step, tile, rows] = zeros
                    pos[1, 1, buffer_step, tile, rows] = zeros
        else:
            store_moved(1, rows, (x, zeros), (y, zeros))
        for step in range(4):
            stiff[step, 0, rows], stiff[step, 1, rows] = ahead(k, zeros, step)
        for step in range(3):
            flags[step, 0, rows], flags[step, 1, rows] = ahead(f, no_flags, step)

    lax.fori_loop(2, 14, set_up, 0)

    def set_coefs(index, carry):
        start = pl.multiple_of(8 * index, 8)
        rows = pl.ds(start, 8)
        for tile in range(2):
            itself = stiff[0, tile, rows]
            bits = flags[0, tile, rows]
            for j, (row_step, col_step, bit, far) in enumerate(BONDS):
                there = pl.ds(start + row_step, 8)
                word = flags[col_step, tile, there] if far else bits
                value = (0.5 * TIME_STEP) * (itself + stiff[col_step, tile, there])
                coef[j, tile, rows] = jnp.where((word & (1 << bit)) != 0, value, 0.0)
        return carry

    lax.fori_loop(1, 15, set_coefs, 0)

    CH = 16

    def forces(buffer, start):
        rows = pl.ds(start, CH)
        for tile in range(2):
            x, y = pos[buffer, 0, 0, tile, rows], pos[buffer, 1, 0, tile, rows]
            from_row = {row_step: x - float(row_step) if row_step else x for row_step in range(-2, 4)}
            sum_x = sum_y = None
            for j, (row_step, col_step, _, _) in enumerate(BONDS):
                there = pl.ds(start + row_step, CH)
                dx = pos[buffer, 0, col_step, tile, there] - from_row[row_step]
                dy = pos[buffer, 1, col_step, tile, there] - y
                square = jnp.maximum(dx * dx + dy * dy, TINY)
                inverse_length = 1.0 / math.sqrt(row_step * row_step + col_step * col_step)
                weight = coef[j, tile, rows] * (inverse_length - lax.rsqrt(square))
                fx, fy = weight * dx, weight * dy
                pair[j, 0, tile, rows] = fx
                pair[j, 1, tile, rows] = fy
                sum_x = fx if sum_x is None else sum_x + fx
                sum_y = fy if sum_y is None else sum_y + fy
            near_sum[0, tile, rows] = sum_x
            near_sum[1, tile, rows] = sum_y

    def move(buffer, scale, start):
        rows = pl.ds(start, CH)
        new = []
        for component in range(2):
            total = [near_sum[component, 0, rows], near_sum[component, 1, rows]]
            for col_step in range(4):
                sums = []
                for tile in range(2):
                    part = None
                    for j, (row_step, step, _, _) in enumerate(BONDS):
                        if step == col_step:
                            value = pair[j, component, tile, pl.ds(start - row_step, CH)]
                            part = value if part is None else part + value
                    sums.append(part)
                back = behind(sums[0], sums[1], col_step)
                total = [total[0] - back[0], total[1] - back[1]]
            moved = []
            for tile in range(2):
                speed = half[component, tile, rows] + scale * (total[tile] + push[component, tile, rows])
                half[component, tile, rows] = speed
                moved.append(pos[buffer, component, 0, tile, rows] + TIME_STEP * speed)
            new.append(moved)
        store_moved(1 - buffer, rows, new[0], new[1])

    def advance(k, carry):
        buffer = lax.rem(k, 2)
        scale = jnp.where((k == 0) | (k == STEPS), 0.5, 1.0).astype(jnp.float32)
        first, last = (15 + 3 * k) // 8, (111 - 3 * k) // 8 + 1
        count = (last - first + 1) // 2

        def force_chunk(i, c):
            forces(buffer, pl.multiple_of(8 * (first + 2 * i), 8))
            return c

        lax.fori_loop(0, count, force_chunk, 0)
        first, last = (18 + 3 * k) // 8, (109 - 3 * k) // 8 + 1
        count = (last - first + 1) // 2

        def move_chunk(i, c):
            move(buffer, scale, pl.multiple_of(8 * (first + 2 * i), 8))
            return c

        lax.fori_loop(0, count, move_chunk, 0)
        return carry

    lax.fori_loop(0, STEPS + 1, advance, 0)
    own = pl.ds(BASE, ROWS)
    for component in range(2):
        disp_out[component] = pos[STEPS % 2, component, 0, 0, own]
        vel_out[component] = half[component, 0, own]


def run_steps(ext, left, right):
    vmem = pl.BlockSpec(memory_space=pltpu.VMEM)
    out = jax.ShapeDtypeStruct((2, ROWS, COLS), jnp.float32)
    return pl.pallas_call(
        steps_kernel,
        out_shape=(out, out),
        in_specs=[vmem] * 3,
        out_specs=(vmem, vmem),
        scratch_shapes=[
            pltpu.VMEM((2, 2, 4, 2, TALL, COLS), jnp.float32),
            pltpu.VMEM((2, 2, TALL, COLS), jnp.float32),
            pltpu.VMEM((2, 2, TALL, COLS), jnp.float32),
            pltpu.VMEM((14, 2, TALL, COLS), jnp.float32),
            pltpu.VMEM((14, 2, 2, TALL, COLS), jnp.float32),
            pltpu.VMEM((2, 2, TALL, COLS), jnp.float32),
            pltpu.VMEM((4, 2, TALL, COLS), jnp.float32),
            pltpu.VMEM((3, 2, TALL, COLS), jnp.int32),
        ],
        compiler_params=pltpu.CompilerParams(vmem_limit_bytes=32 * 1024 * 1024),
        name="steps",
    )(*(pltpu.with_memory_space_constraint(a, pltpu.VMEM) for a in (ext, left, right)))


def solution(mesh):
    shape_x, shape_y = mesh.shape["gx"], mesh.shape["gy"]

    def on_device(disp, vel, stiffness, body_force, bond_bits):
        halos = exchange(shape_x, shape_y, disp, vel, stiffness, body_force, bond_bits)
        return run_steps(*halos)

    plane, word = P("gx", "gy"), P(None, "gx", "gy")
    return jax.shard_map(
        on_device, mesh=mesh, in_specs=(word, word, plane, word, word), out_specs=(word, word), check_vma=False
    )
```

time: 248 us -> 43.1 us (0.17)
  the two profiles are of different devices: /device:TPU:397 before, /device:TPU:1 now
where the time goes in v1:
time: 43.1 us; the launch traced here: 42.9 us
  Pallas kernels  42.2 us (98%)
  between operations  0.64 us (1%)
    pallas_call x1, Pallas kernels, exchange(): pl.pallas_call(functools.partial(exchange_kernel, shape_x, shape_y), out_...  23.6 us
    pallas_call x1, Pallas kernels, run_steps(): pl.pallas_call(steps_kernel, out_shape=(out, out), in_specs=[vmem] * 3, o...  18.7 us

profile of v1, /device:TPU:1, one launch (start us, length us, event | category | flops | bytes accessed | tf_op | source)
XLA Modules:
  0.0 42.9 jit_solution(6702705470707687507)
XLA Ops:
  0.6 23.6 %exchange.1 = (f32[8,128,128]{2,1,0:T(8,128)S(1)}, f32[2,96,128]{2,1,0:T(8,128)S(1)}, f32[2,96,128]{2,1,0:T(8,128)S(1)}) custom-call(f32[2,32,128]{2,1,0:T(8,128)} %disp.1, f32[2,32,128]{2,1,0:T(8,128)} %vel.1, f32[32,128]{1,0:T(8,128)} %stiff.1, f32[2,32,128]{2,1,0:T(8,128)} %body.1, s32[2,32,128]{2,1,0:T(8,128)} %bits.1), custom_call_target="tpu_custom_call" | custom-call | tf_op jit(solution)/shard_map/exchange/pallas_call | solution.py:154
  24.2 18.7 %steps.1 = (f32[2,32,128]{2,1,0:T(8,128)}, f32[2,32,128]{2,1,0:T(8,128)}) custom-call(f32[8,128,128]{2,1,0:T(8,128)S(1)} %get-tuple-element.5.ext, f32[2,96,128]{2,1,0:T(8,128)S(1)} %get-tuple-element.6.left, f32[2,96,128]{2,1,0:T(8,128)S(1)} %get-tuple-element.7.right), custom_call_target="tpu_custom_call" | custom-call | tf_op jit(solution)/shard_map/steps/pallas_call | solution.py:337

commit v2 on v0

v2 whole, which is shorter than its diff:
```python
import functools
import math

import jax
import jax.numpy as jnp
from jax import lax
from jax.experimental import pallas as pl
from jax.experimental.pallas import tpu as pltpu
from jax.sharding import PartitionSpec as P

STEPS = 10
TIME_STEP = 0.04
ROWS = 32
COLS = 128
BASE = 48
TALL = 128
SIDE = 96
TINY = 1.2e-38
MESH = pl.DeviceIdType.MESH
OWN = pl.ds(BASE, ROWS)
GROUPS = [0, 32, 64, 96]


def upper_shell():
    upper = []
    for row_step in range(0, 4):
        for col_step in range(-3, 4):
            if row_step * row_step + col_step * col_step <= 9 and (row_step > 0 or col_step > 0):
                upper.append((row_step, col_step))
    return upper


def half_shell():
    bonds = []
    for index, (row_step, col_step) in enumerate(upper_shell()):
        if col_step >= 0:
            bonds.append((row_step, col_step, index, False))
        else:
            bonds.append((-row_step, -col_step, index, True))
    return sorted(bonds, key=lambda bond: (bond[1], bond[0]))


BONDS = half_shell()


def lanes_of(shape):
    return lax.broadcasted_iota(jnp.int32, shape, len(shape) - 1)


def ahead(first, second, step):
    inside = lanes_of(first.shape) < COLS - step
    a, b = pltpu.roll(first, COLS - step, 1), pltpu.roll(second, COLS - step, 1)
    return jnp.where(inside, a, b), jnp.where(inside, b, a)


def behind(first, second, step):
    if step == 0:
        return first, second
    inside = lanes_of(first.shape) >= step
    a, b = pltpu.roll(first, step, 1), pltpu.roll(second, step, 1)
    return jnp.where(inside, a, b), jnp.where(inside, b, a)


def spread(pos, start, chunk):
    rows = pl.ds(start, chunk)
    for component in range(2):
        first, second = pos[component, 0, 0, rows], pos[component, 0, 1, rows]
        for step in range(1, 4):
            a, b = ahead(first, second, step)
            pos[component, step, 0, rows] = a + float(step) if component else a
            pos[component, step, 1, rows] = b + float(step) if component else b


def forces(pos, coef, pair, near_sum, start, chunk):
    rows = pl.ds(start, chunk)
    for tile in range(2):
        x, y = pos[0, 0, tile, rows], pos[1, 0, tile, rows]
        from_row = {row_step: x - float(row_step) if row_step else x for row_step in range(-2, 4)}
        sum_x = sum_y = None
        for j, (row_step, col_step, _, _) in enumerate(BONDS):
            there = pl.ds(start + row_step, chunk)
            dx = pos[0, col_step, tile, there] - from_row[row_step]
            dy = pos[1, col_step, tile, there] - y
            square = jnp.maximum(dx * dx + dy * dy, TINY)
            inverse_length = 1.0 / math.sqrt(row_step * row_step + col_step * col_step)
            weight = coef[j, tile, rows] * (inverse_length - lax.rsqrt(square))
            fx, fy = weight * dx, weight * dy
            pair[j, 0, tile, rows] = fx
            pair[j, 1, tile, rows] = fy
            sum_x = fx if sum_x is None else sum_x + fx
            sum_y = fy if sum_y is None else sum_y + fy
        near_sum[0, tile, rows] = sum_x
        near_sum[1, tile, rows] = sum_y


def force_loop(k, pos, coef, pair, near_sum):
    first, last = (15 + 3 * k) // 8, (111 - 3 * k) // 8 + 1

    def force_chunk(i, carry):
        forces(pos, coef, pair, near_sum, pl.multiple_of(8 * (first + 2 * i), 8), 16)
        return carry

    lax.fori_loop(0, (last - first + 1) // 2, force_chunk, 0)


def move(pos, pair, near_sum, push, half, scale, start, chunk):
    rows = pl.ds(start, chunk)
    for component in range(2):
        total = [near_sum[component, 0, rows], near_sum[component, 1, rows]]
        for col_step in range(4):
            sums = []
            for tile in range(2):
                part = None
                for j, (row_step, step, _, _) in enumerate(BONDS):
                    if step == col_step:
                        value = pair[j, component, tile, pl.ds(start - row_step, chunk)]
                        part = value if part is None else part + value
                sums.append(part)
            back = behind(sums[0], sums[1], col_step)
            total = [total[0] - back[0], total[1] - back[1]]
        for tile in range(2):
            speed = half[component, tile, rows] + scale * (total[tile] + push[component, tile, rows])
            half[component, tile, rows] = speed
            pos[component, 0, tile, rows] = pos[component, 0, tile, rows] + TIME_STEP * speed


def packed(fields, start):
    lanes = lanes_of((ROWS, COLS))
    total = None
    for field, group in zip(fields, GROUPS, strict=True):
        moved = pltpu.roll(field, (group - start) % COLS, 1)
        total = moved if total is None else jnp.where((lanes >= group) & (lanes < group + 32), moved, total)
    return total


def beside(right, left, word, group, rows):
    from_right = pltpu.roll(right[word, rows], (-32 * group) % COLS, 1)
    from_left = pltpu.roll(left[word, rows], (96 - 32 * group) % COLS, 1)
    return from_right, from_left


def set_up(near, left, right, pos, coef, stiff, flags):
    lanes8 = lanes_of((8, COLS))
    zeros = jnp.zeros((8, COLS), jnp.float32)
    for index in range(1, 15):
        rows = pl.ds(8 * index, 8)
        x, y, k, bits = (near[field, rows] for field in range(4))
        pos[0, 0, 0, rows] = x
        pos[1, 0, 0, rows] = y
        stiff[0, 0, rows] = k
        flags[0, 0, rows] = bits.astype(jnp.int32)
        others = [zeros] * 4
        if 2 <= index < 14:
            side = pl.ds(8 * index - 16, 8)
            for field in range(4):
                from_right, from_left = beside(right, left, 0, field, side)
                value = jnp.where(lanes8 < 32, from_right, jnp.where(lanes8 >= 96, from_left, 0.0))
                if 6 <= index < 10:
                    far_right = pltpu.roll(right[1, side], (32 - (32 * field + 30)) % COLS, 1)
                    far_left = pltpu.roll(left[1, side], (95 - (32 * field + 1)) % COLS, 1)
                    value = jnp.where(lanes8 == 32, far_right, jnp.where(lanes8 == 95, far_left, value))
                others[field] = value
        pos[0, 0, 1, rows] = others[0]
        pos[1, 0, 1, rows] = others[1]
        stiff[0, 1, rows] = others[2]
        flags[0, 1, rows] = others[3].astype(jnp.int32)
    for index in range(1, 15):
        rows = pl.ds(8 * index, 8)
        for step in range(1, 4):
            stiff[step, 0, rows], stiff[step, 1, rows] = ahead(stiff[0, 0, rows], stiff[0, 1, rows], step)
        for step in range(1, 3):
            flags[step, 0, rows], flags[step, 1, rows] = ahead(flags[0, 0, rows], flags[0, 1, rows], step)
        spread(pos, 8 * index, 8)

    def set_coefs(index, carry):
        start = pl.multiple_of(8 * index, 8)
        rows = pl.ds(start, 8)
        for tile in range(2):
            itself = stiff[0, tile, rows]
            bits = flags[0, tile, rows]
            for j, (row_step, col_step, bit, far) in enumerate(BONDS):
                there = pl.ds(start + row_step, 8)
                word = flags[col_step, tile, there] if far else bits
                value = 0.5 * (itself + stiff[col_step, tile, there])
                coef[j, tile, rows] = jnp.where((word & (1 << bit)) != 0, value, 0.0)
        return carry

    lax.fori_loop(1, 15, set_coefs, 0)


def exchange_kernel(shape_x, shape_y, disp, vel, stiff_own, body, bits, half, push, pos, coef, pair, near_sum,
                    near, left, right, stiff, flags, bits_own, to_west, to_east, local_sem, send_sem, recv_sem):
    gx, gy = lax.axis_index("gx"), lax.axis_index("gy")

    def neighbour(row_step, col_step):
        return (
            lax.rem(gx + row_step + shape_x, shape_x),
            lax.rem(gy + col_step + shape_y, shape_y),
        )

    around = [(-1, 0), (1, 0), (0, -1), (0, 1), (-1, -1), (-1, 1), (1, -1), (1, 1), (-2, 0), (2, 0)]
    barrier = pltpu.get_barrier_semaphore()
    for step in around:
        pl.semaphore_signal(barrier, inc=1, device_id=neighbour(*step), device_id_type=MESH)

    local = [
        pltpu.make_async_copy(bits.at[0], bits_own, local_sem.at[0]),
        pltpu.make_async_copy(disp, near.at[pl.ds(0, 2), OWN], local_sem.at[1]),
        pltpu.make_async_copy(stiff_own, near.at[2, OWN], local_sem.at[2]),
        pltpu.make_async_copy(vel, half.at[:, 0, OWN], local_sem.at[3]),
        pltpu.make_async_copy(body, push.at[:, 0, OWN], local_sem.at[4]),
    ]
    for copy in local:
        copy.start()
    zeros = jnp.zeros((8, COLS), jnp.float32)
    for index in (0, 15):
        rows = pl.ds(8 * index, 8)
        for step in range(4):
            for tile in range(2):
                pos[0, step, tile, rows] = zeros
                pos[1, step, tile, rows] = zeros
                stiff[step, tile, rows] = zeros
        for step in range(3):
            for tile in range(2):
                flags[step, tile, rows] = jnp.zeros((8, COLS), jnp.int32)
    for copy in local:
        copy.wait()
    near[3, OWN] = bits_own[...].astype(jnp.float32)

    first_four = [near[field, OWN] for field in range(4)]
    last_four = [half[0, 0, OWN], half[1, 0, OWN], push[0, 0, OWN], push[1, 0, OWN]]
    lanes = lanes_of((ROWS, COLS))
    to_west[0] = packed(first_four, 0)
    to_east[0] = packed(first_four, 96)
    west, east = packed(last_four, 0), packed(last_four, 96)
    for field in range(4):
        group = GROUPS[field]
        west = jnp.where(lanes == group + 30, pltpu.roll(first_four[field], (group + 30 - 32) % COLS, 1), west)
        east = jnp.where(lanes == group + 1, pltpu.roll(first_four[field], (group + 1 - 95) % COLS, 1), east)
    to_west[1] = west
    to_east[1] = east

    pl.semaphore_wait(barrier, len(around))

    four = pl.ds(0, 4)
    plan = [
        (near.at[four, OWN], near.at[four, pl.ds(BASE + ROWS, ROWS)], (-1, 0)),
        (near.at[four, OWN], near.at[four, pl.ds(BASE - ROWS, ROWS)], (1, 0)),
        (to_west, right.at[:, pl.ds(64, 32)], (-1, -1)),
        (to_east, left.at[:, pl.ds(64, 32)], (-1, 1)),
        (to_west, right.at[:, pl.ds(0, 32)], (1, -1)),
        (to_east, left.at[:, pl.ds(0, 32)], (1, 1)),
        (to_west, right.at[:, pl.ds(32, 32)], (0, -1)),
        (to_east, left.at[:, pl.ds(32, 32)], (0, 1)),
        (near.at[four, pl.ds(BASE, 8)], near.at[four, pl.ds(BASE + 64, 8)], (-2, 0)),
        (near.at[four, pl.ds(BASE + 24, 8)], near.at[four, pl.ds(BASE - 40, 8)], (2, 0)),
        (half.at[:, 0, OWN], half.at[:, 0, pl.ds(BASE + ROWS, ROWS)], (-1, 0)),
        (half.at[:, 0, OWN], half.at[:, 0, pl.ds(BASE - ROWS, ROWS)], (1, 0)),
        (push.at[:, 0, OWN], push.at[:, 0, pl.ds(BASE + ROWS, ROWS)], (-1, 0)),
        (push.at[:, 0, OWN], push.at[:, 0, pl.ds(BASE - ROWS, ROWS)], (1, 0)),
    ]
    copies = [
        pltpu.make_async_remote_copy(
            src_ref=source,
            dst_ref=target,
            send_sem=send_sem.at[index],
            recv_sem=recv_sem.at[index],
            device_id=neighbour(*step),
            device_id_type=MESH,
        )
        for index, (source, target, step) in enumerate(plan)
    ]
    order = [2, 3, 4, 5, 0, 1, 6, 7, 8, 9]
    for index in order:
        copies[index].start()
    for index in (0, 1):
        copies[index].wait_send()
    for copy in copies[10:]:
        copy.start()
    for copy in copies[:10]:
        copy.wait_recv()
    set_up(near, left, right, pos, coef, stiff, flags)
    force_loop(0, pos, coef, pair, near_sum)
    lanes8 = lanes_of((8, COLS))
    for index in range(2, 14):
        rows = pl.ds(8 * index, 8)
        side = pl.ds(8 * index - 16, 8)
        for field in range(4):
            from_right, from_left = beside(right, left, 1, field, side)
            value = jnp.where(lanes8 < 30, from_right, jnp.where(lanes8 >= 98, from_left, 0.0))
            (half if field < 2 else push)[field % 2, 1, rows] = value
    for copy in copies[10:]:
        copy.wait_recv()
    for copy in copies[2:]:
        copy.wait_send()


F32 = jnp.float32
POS = (2, 4, 2, TALL, COLS)
PAIR = (14, 2, 2, TALL, COLS)
SUM = (2, 2, TALL, COLS)


def exchange(shape_x, shape_y, *args):
    hbm = pl.BlockSpec(memory_space=pltpu.HBM)
    vmem = pl.BlockSpec(memory_space=pltpu.VMEM)
    shapes = (SUM, SUM, POS, (14, 2, TALL, COLS), PAIR, SUM)
    return pl.pallas_call(
        functools.partial(exchange_kernel, shape_x, shape_y),
        out_shape=tuple(pltpu.VMEM(shape, F32) for shape in shapes),
        in_specs=[hbm] * 5,
        out_specs=(vmem,) * len(shapes),
        scratch_shapes=[
            pltpu.VMEM((4, TALL, COLS), F32),
            pltpu.VMEM((2, SIDE, COLS), F32),
            pltpu.VMEM((2, SIDE, COLS), F32),
            pltpu.VMEM((4, 2, TALL, COLS), F32),
            pltpu.VMEM((3, 2, TALL, COLS), jnp.int32),
            pltpu.VMEM((ROWS, COLS), jnp.int32),
            pltpu.VMEM((2, ROWS, COLS), F32),
            pltpu.VMEM((2, ROWS, COLS), F32),
            pltpu.SemaphoreType.DMA((5,)),
            pltpu.SemaphoreType.DMA((14,)),
            pltpu.SemaphoreType.DMA((14,)),
        ],
        compiler_params=pltpu.CompilerParams(
            collective_id=0, has_side_effects=True, vmem_limit_bytes=24 * 1024 * 1024
        ),
        name="exchange",
    )(*(pltpu.with_memory_space_constraint(a, pltpu.HBM) for a in args))


def region(k):
    return (18 + 3 * k) // 8, (109 - 3 * k) // 8 + 1


def steps_kernel(push, coef, half_in, pos_in, pair_in, sum_in, disp_out, vel_out, half, pos, pair, near_sum):
    del half_in, pos_in, pair_in, sum_in
    k = 0
    while k < STEPS:
        first, last = region(k)
        end = k + 1
        while end < STEPS and region(end) == (first, last):
            end += 1

        def advance(step, carry, starting=k == 0, first=first, last=last):
            scale = jnp.where(step == 0, 0.5 * TIME_STEP, TIME_STEP).astype(F32) if starting else TIME_STEP
            for index in range(first, last, 2):
                move(pos, pair, near_sum, push, half, scale, 8 * index, 16)
            for index in range(first, last, 2):
                spread(pos, 8 * index, 16)
            for index in range(first, last, 2):
                forces(pos, coef, pair, near_sum, 8 * index, 16)
            return carry

        lax.fori_loop(k, end, advance, 0)
        k = end
    for component in range(2):
        disp_out[component] = pos[component, 0, 0, OWN]
    first, last = region(STEPS)
    for index in range(first, last, 2):
        move(pos, pair, near_sum, push, half, 0.5 * TIME_STEP, 8 * index, 16)
    for component in range(2):
        vel_out[component] = half[component, 0, OWN]


def run_steps(half, push, pos, coef, pair, near_sum):
    vmem = pl.BlockSpec(memory_space=pltpu.VMEM)
    out = jax.ShapeDtypeStruct((2, ROWS, COLS), F32)
    arrays = (push, coef, half, pos, pair, near_sum)
    return pl.pallas_call(
        steps_kernel,
        out_shape=(out, out, *(pltpu.VMEM(shape, F32) for shape in (SUM, POS, PAIR, SUM))),
        in_specs=[vmem] * len(arrays),
        out_specs=(vmem,) * 6,
        input_output_aliases={2: 2, 3: 3, 4: 4, 5: 5},
        compiler_params=pltpu.CompilerParams(vmem_limit_bytes=24 * 1024 * 1024),
        name="steps",
    )(*(pltpu.with_memory_space_constraint(a, pltpu.VMEM) for a in arrays))[:2]


def solution(mesh):
    shape_x, shape_y = mesh.shape["gx"], mesh.shape["gy"]

    def on_device(disp, vel, stiffness, body_force, bond_bits):
        started = exchange(shape_x, shape_y, disp, vel, stiffness, body_force, bond_bits)
        return run_steps(*started)

    plane, word = P("gx", "gy"), P(None, "gx", "gy")
    return jax.shard_map(
        on_device, mesh=mesh, in_specs=(word, word, plane, word, word), out_specs=(word, word), check_vma=False
    )
```

time: 248 us -> 33.1 us (0.13)
  the two profiles are of different devices: /device:TPU:397 before, /device:TPU:1 now
where the time goes in v2:
time: 33.1 us; the launch traced here: 32.9 us
  Pallas kernels  32.2 us (97%)
  between operations  0.64 us (2%)
    pallas_call x1, Pallas kernels, exchange(): pl.pallas_call(functools.partial(exchange_kernel, shape_x, shape_y), out_...  24 us
    pallas_call x1, Pallas kernels, run_steps(): pl.pallas_call(steps_kernel, out_shape=(out, out, *(pltpu.VMEM(shape, F32...  8.23 us

profile of v2, /device:TPU:1, one launch (start us, length us, event | category | flops | bytes accessed | tf_op | source)
XLA Modules:
  0.0 32.9 jit_solution(665927133491672319)
XLA Ops:
  0.6 24.0 %exchange.1 = (f32[2,2,128,128]{3,2,1,0:T(8,128)S(1)}, f32[2,2,128,128]{3,2,1,0:T(8,128)S(1)}, f32[2,4,2,128,128]{4,3,2,1,0:T(8,128)S(1)}, f32[14,2,128,128]{3,2...) custom-call(f32[2,32,128]{2,1,0:T(8,128)} %disp.1, f32[2,32,128]{2,1,0:T(8,128)} %vel.1, ...), custom_call_target="tpu_custom_call" | custom-call | tf_op jit(solution)/shard_map/exchange/pallas_call | solution.py:308
  24.6 8.2 %steps.1 = (f32[2,32,128]{2,1,0:T(8,128)}, f32[2,32,128]{2,1,0:T(8,128)}, f32[2,2,128,128]{3,2,1,0:T(8,128)S(1)}, f32[2,4,2,128,128]{4,3,2,1,0:T(8,128)S(1)}, f3...) custom-call(f32[2,2,128,128]{3,2,1,0:T(8,128)S(1)} %get-tuple-elemen, ...), custom_call_target="tpu_custom_call", output_to_operand_aliasing={{2}: (2, {}), {3}: (3, {}), {4}: (4, {}), {5}: (5, {})} | custom-call | tf_op jit(solution)/shard_map/steps/pallas_call | solution.py:371

commit v3 on v2

--- a/solution.py
+++ b/solution.py
@@ -18,7 +18,8 @@
 TINY = 1.2e-38
 MESH = pl.DeviceIdType.MESH
 OWN = pl.ds(BASE, ROWS)
-GROUPS = [0, 32, 64, 96]
+WEST = [0, 32, 64, 96]
+EAST = [96, 0, 32, 64]
 
 
 def upper_shell():
@@ -103,7 +104,7 @@
     lax.fori_loop(0, (last - first + 1) // 2, force_chunk, 0)
 
 
-def move(pos, pair, near_sum, push, half, scale, start, chunk):
+def move(pos, pair, near_sum, flow, scale, start, chunk, last=False):
     rows = pl.ds(start, chunk)
     for component in range(2):
         total = [near_sum[component, 0, rows], near_sum[component, 1, rows]]
@@ -118,59 +119,82 @@
                 sums.append(part)
             back = behind(sums[0], sums[1], col_step)
             total = [total[0] - back[0], total[1] - back[1]]
-        for tile in range(2):
-            speed = half[component, tile, rows] + scale * (total[tile] + push[component, tile, rows])
-            half[component, tile, rows] = speed
-            pos[component, 0, tile, rows] = pos[component, 0, tile, rows] + TIME_STEP * speed
-
-
-def packed(fields, start):
+        for tile in range(1 if last else 2):
+            speed = flow[component, tile, rows] + scale * (total[tile] + flow[2 + component, tile, rows])
+            flow[component, tile, rows] = speed
+            if not last:
+                pos[component, 0, tile, rows] = pos[component, 0, tile, rows] + TIME_STEP * speed
+
+
+def packed(fields, start, groups):
     lanes = lanes_of((ROWS, COLS))
     total = None
-    for field, group in zip(fields, GROUPS, strict=True):
-        moved = pltpu.roll(field, (group - start) % COLS, 1)
+    for field, group in zip(fields, groups, strict=True):
+        moved = pltpu.roll(field, (group - start) % COLS, 1) if group != start else field
         total = moved if total is None else jnp.where((lanes >= group) & (lanes < group + 32), moved, total)
     return total
 
 
-def beside(right, left, word, group, rows):
-    from_right = pltpu.roll(right[word, rows], (-32 * group) % COLS, 1)
-    from_left = pltpu.roll(left[word, rows], (96 - 32 * group) % COLS, 1)
-    return from_right, from_left
-
-
-def set_up(near, left, right, pos, coef, stiff, flags):
+def beside(right, left, word, field, rows):
+    lanes = lanes_of((8, COLS))
+    at_right, at_left = WEST[field], EAST[field]
+    value = jnp.where((lanes >= at_left) & (lanes < at_left + 32), left[word, rows], 0.0)
+    value = jnp.where((lanes >= at_right) & (lanes < at_right + 32), right[word, rows], value)
+    return pltpu.roll(value, -at_right % COLS, 1) if at_right else value
+
+
+def begin(near, pos, stiff, flags, tiles):
+    for index in tiles:
+        rows = pl.ds(8 * index, 8)
+        x, y, k = (near[field, rows] for field in range(3))
+        bits = near[3, rows].astype(jnp.int32)
+        pos[0, 0, 0, rows] = x
+        pos[1, 0, 0, rows] = y
+        stiff[0, 0, rows] = k
+        flags[0, 0, rows] = bits
+        for step in range(1, 4):
+            pos[0, step, 0, rows] = pltpu.roll(x, COLS - step, 1)
+            pos[1, step, 0, rows] = pltpu.roll(y, COLS - step, 1)
+            stiff[step, 0, rows] = pltpu.roll(k, COLS - step, 1)
+        for step in range(1, 3):
+            flags[step, 0, rows] = pltpu.roll(bits, COLS - step, 1)
+
+
+def finish(left, right, pos, coef, stiff, flags):
     lanes8 = lanes_of((8, COLS))
     zeros = jnp.zeros((8, COLS), jnp.float32)
     for index in range(1, 15):
         rows = pl.ds(8 * index, 8)
-        x, y, k, bits = (near[field, rows] for field in range(4))
-        pos[0, 0, 0, rows] = x
-        pos[1, 0, 0, rows] = y
-        stiff[0, 0, rows] = k
-        flags[0, 0, rows] = bits.astype(jnp.int32)
         others = [zeros] * 4
         if 2 <= index < 14:
             side = pl.ds(8 * index - 16, 8)
             for field in range(4):
-                from_right, from_left = beside(right, left, 0, field, side)
-                value = jnp.where(lanes8 < 32, from_right, jnp.where(lanes8 >= 96, from_left, 0.0))
+                value = beside(right, left, 0, field, side)
                 if 6 <= index < 10:
-                    far_right = pltpu.roll(right[1, side], (32 - (32 * field + 30)) % COLS, 1)
-                    far_left = pltpu.roll(left[1, side], (95 - (32 * field + 1)) % COLS, 1)
+                    far_right = pltpu.roll(right[1, side], (32 - (WEST[field] + 30)) % COLS, 1)
+                    far_left = pltpu.roll(left[1, side], (95 - (EAST[field] + 1)) % COLS, 1)
                     value = jnp.where(lanes8 == 32, far_right, jnp.where(lanes8 == 95, far_left, value))
                 others[field] = value
         pos[0, 0, 1, rows] = others[0]
         pos[1, 0, 1, rows] = others[1]
         stiff[0, 1, rows] = others[2]
         flags[0, 1, rows] = others[3].astype(jnp.int32)
+
+    def complete(ref, where, step, rows, bias):
+        inside = lanes8 < COLS - step
+        own, other = ref[(*where, step, 0, rows)], pltpu.roll(ref[(*where, 0, 1, rows)], COLS - step, 1)
+        first, second = jnp.where(inside, own, other), jnp.where(inside, other, own)
+        ref[(*where, step, 0, rows)] = first + bias if bias else first
+        ref[(*where, step, 1, rows)] = second + bias if bias else second
+
     for index in range(1, 15):
         rows = pl.ds(8 * index, 8)
         for step in range(1, 4):
-            stiff[step, 0, rows], stiff[step, 1, rows] = ahead(stiff[0, 0, rows], stiff[0, 1, rows], step)
+            complete(pos, (0,), step, rows, 0.0)
+            complete(pos, (1,), step, rows, float(step))
+            complete(stiff, (), step, rows, 0.0)
         for step in range(1, 3):
-            flags[step, 0, rows], flags[step, 1, rows] = ahead(flags[0, 0, rows], flags[0, 1, rows], step)
-        spread(pos, 8 * index, 8)
+            complete(flags, (), step, rows, 0)
 
     def set_coefs(index, carry):
         start = pl.multiple_of(8 * index, 8)
@@ -188,7 +212,7 @@
     lax.fori_loop(1, 15, set_coefs, 0)
 
 
-def exchange_kernel(shape_x, shape_y, disp, vel, stiff_own, body, bits, half, push, pos, coef, pair, near_sum,
+def exchange_kernel(shape_x, shape_y, disp, vel, stiff_own, body, bits, flow, pos, coef, pair, near_sum,
                     near, left, right, stiff, flags, bits_own, to_west, to_east, local_sem, send_sem, recv_sem):
     gx, gy = lax.axis_index("gx"), lax.axis_index("gy")
 
@@ -198,7 +222,7 @@
             lax.rem(gy + col_step + shape_y, shape_y),
         )
 
-    around = [(-1, 0), (1, 0), (0, -1), (0, 1), (-1, -1), (-1, 1), (1, -1), (1, 1), (-2, 0), (2, 0)]
+    around = [(-1, -1), (-1, 1), (1, -1), (1, 1), (-1, 0), (1, 0), (0, -1), (0, 1), (-2, 0), (2, 0)]
     barrier = pltpu.get_barrier_semaphore()
     for step in around:
         pl.semaphore_signal(barrier, inc=1, device_id=neighbour(*step), device_id_type=MESH)
@@ -207,8 +231,8 @@
         pltpu.make_async_copy(bits.at[0], bits_own, local_sem.at[0]),
         pltpu.make_async_copy(disp, near.at[pl.ds(0, 2), OWN], local_sem.at[1]),
         pltpu.make_async_copy(stiff_own, near.at[2, OWN], local_sem.at[2]),
-        pltpu.make_async_copy(vel, half.at[:, 0, OWN], local_sem.at[3]),
-        pltpu.make_async_copy(body, push.at[:, 0, OWN], local_sem.at[4]),
+        pltpu.make_async_copy(vel, flow.at[pl.ds(0, 2), 0, OWN], local_sem.at[3]),
+        pltpu.make_async_copy(body, flow.at[pl.ds(2, 2), 0, OWN], local_sem.at[4]),
     ]
     for copy in local:
         copy.start()
@@ -228,17 +252,18 @@
     near[3, OWN] = bits_own[...].astype(jnp.float32)
 
     first_four = [near[field, OWN] for field in range(4)]
-    last_four = [half[0, 0, OWN], half[1, 0, OWN], push[0, 0, OWN], push[1, 0, OWN]]
+    last_four = [flow[field, 0, OWN] for field in range(4)]
     lanes = lanes_of((ROWS, COLS))
-    to_west[0] = packed(first_four, 0)
-    to_east[0] = packed(first_four, 96)
-    west, east = packed(last_four, 0), packed(last_four, 96)
+    to_west[0] = packed(first_four, 0, WEST)
+    to_east[0] = packed(first_four, 96, EAST)
+    west, east = packed(last_four, 0, WEST), packed(last_four, 96, EAST)
     for field in range(4):
-        group = GROUPS[field]
-        west = jnp.where(lanes == group + 30, pltpu.roll(first_four[field], (group + 30 - 32) % COLS, 1), west)
-        east = jnp.where(lanes == group + 1, pltpu.roll(first_four[field], (group + 1 - 95) % COLS, 1), east)
+        at_west, at_east = WEST[field] + 30, EAST[field] + 1
+        west = jnp.where(lanes == at_west, pltpu.roll(first_four[field], (at_west - 32) % COLS, 1), west)
+        east = jnp.where(lanes == at_east, pltpu.roll(first_four[field], (at_east - 95) % COLS, 1), east)
     to_west[1] = west
     to_east[1] = east
+    begin(near, pos, stiff, flags, range(6, 10))
 
     pl.semaphore_wait(barrier, len(around))
 
@@ -246,18 +271,20 @@
     plan = [
         (near.at[four, OWN], near.at[four, pl.ds(BASE + ROWS, ROWS)], (-1, 0)),
         (near.at[four, OWN], near.at[four, pl.ds(BASE - ROWS, ROWS)], (1, 0)),
-        (to_west, right.at[:, pl.ds(64, 32)], (-1, -1)),
-        (to_east, left.at[:, pl.ds(64, 32)], (-1, 1)),
-        (to_west, right.at[:, pl.ds(0, 32)], (1, -1)),
-        (to_east, left.at[:, pl.ds(0, 32)], (1, 1)),
+        (to_west.at[0], right.at[0, pl.ds(64, 32)], (-1, -1)),
+        (to_east.at[0], left.at[0, pl.ds(64, 32)], (-1, 1)),
+        (to_west.at[0], right.at[0, pl.ds(0, 32)], (1, -1)),
+        (to_east.at[0], left.at[0, pl.ds(0, 32)], (1, 1)),
         (to_west, right.at[:, pl.ds(32, 32)], (0, -1)),
         (to_east, left.at[:, pl.ds(32, 32)], (0, 1)),
         (near.at[four, pl.ds(BASE, 8)], near.at[four, pl.ds(BASE + 64, 8)], (-2, 0)),
         (near.at[four, pl.ds(BASE + 24, 8)], near.at[four, pl.ds(BASE - 40, 8)], (2, 0)),
-        (half.at[:, 0, OWN], half.at[:, 0, pl.ds(BASE + ROWS, ROWS)], (-1, 0)),
-        (half.at[:, 0, OWN], half.at[:, 0, pl.ds(BASE - ROWS, ROWS)], (1, 0)),
-        (push.at[:, 0, OWN], push.at[:, 0, pl.ds(BASE + ROWS, ROWS)], (-1, 0)),
-        (push.at[:, 0, OWN], push.at[:, 0, pl.ds(BASE - ROWS, ROWS)], (1, 0)),
+        (to_west.at[1], right.at[1, pl.ds(64, 32)], (-1, -1)),
+        (to_east.at[1], left.at[1, pl.ds(64, 32)], (-1, 1)),
+        (to_west.at[1], right.at[1, pl.ds(0, 32)], (1, -1)),
+        (to_east.at[1], left.at[1, pl.ds(0, 32)], (1, 1)),
+        (flow.at[:, 0, OWN], flow.at[:, 0, pl.ds(BASE + ROWS, ROWS)], (-1, 0)),
+        (flow.at[:, 0, OWN], flow.at[:, 0, pl.ds(BASE - ROWS, ROWS)], (1, 0)),
     ]
     copies = [
         pltpu.make_async_remote_copy(
@@ -270,26 +297,30 @@
         )
         for index, (source, target, step) in enumerate(plan)
     ]
-    order = [2, 3, 4, 5, 0, 1, 6, 7, 8, 9]
+    order = [2, 3, 4, 5, 0, 1, 6, 7, 8, 9, 10, 11, 12, 13]
     for index in order:
         copies[index].start()
     for index in (0, 1):
         copies[index].wait_send()
-    for copy in copies[10:]:
+    for copy in copies[14:]:
         copy.start()
-    for copy in copies[:10]:
+    for index in (0, 1, 8, 9):
+        copies[index].wait_recv()
+    begin(near, pos, stiff, flags, [*range(1, 6), *range(10, 15)])
+    for copy in copies[2:8]:
         copy.wait_recv()
-    set_up(near, left, right, pos, coef, stiff, flags)
+    finish(left, right, pos, coef, stiff, flags)
     force_loop(0, pos, coef, pair, near_sum)
+    for copy in copies[10:14]:
+        copy.wait_recv()
     lanes8 = lanes_of((8, COLS))
     for index in range(2, 14):
         rows = pl.ds(8 * index, 8)
         side = pl.ds(8 * index - 16, 8)
         for field in range(4):
-            from_right, from_left = beside(right, left, 1, field, side)
-            value = jnp.where(lanes8 < 30, from_right, jnp.where(lanes8 >= 98, from_left, 0.0))
-            (half if field < 2 else push)[field % 2, 1, rows] = value
-    for copy in copies[10:]:
+            value = beside(right, left, 1, field, side)
+            flow[field, 1, rows] = jnp.where((lanes8 < 30) | (lanes8 >= 98), value, 0.0)
+    for copy in copies[14:]:
         copy.wait_recv()
     for copy in copies[2:]:
         copy.wait_send()
@@ -299,12 +330,13 @@
 POS = (2, 4, 2, TALL, COLS)
 PAIR = (14, 2, 2, TALL, COLS)
 SUM = (2, 2, TALL, COLS)
+FLOW = (4, 2, TALL, COLS)
 
 
 def exchange(shape_x, shape_y, *args):
     hbm = pl.BlockSpec(memory_space=pltpu.HBM)
     vmem = pl.BlockSpec(memory_space=pltpu.VMEM)
-    shapes = (SUM, SUM, POS, (14, 2, TALL, COLS), PAIR, SUM)
+    shapes = (FLOW, POS, (14, 2, TALL, COLS), PAIR, SUM)
     return pl.pallas_call(
         functools.partial(exchange_kernel, shape_x, shape_y),
         out_shape=tuple(pltpu.VMEM(shape, F32) for shape in shapes),
@@ -320,8 +352,8 @@
             pltpu.VMEM((2, ROWS, COLS), F32),
             pltpu.VMEM((2, ROWS, COLS), F32),
             pltpu.SemaphoreType.DMA((5,)),
-            pltpu.SemaphoreType.DMA((14,)),
-            pltpu.SemaphoreType.DMA((14,)),
+            pltpu.SemaphoreType.DMA((16,)),
+            pltpu.SemaphoreType.DMA((16,)),
         ],
         compiler_params=pltpu.CompilerParams(
             collective_id=0, has_side_effects=True, vmem_limit_bytes=24 * 1024 * 1024
@@ -334,8 +366,8 @@
     return (18 + 3 * k) // 8, (109 - 3 * k) // 8 + 1
 
 
-def steps_kernel(push, coef, half_in, pos_in, pair_in, sum_in, disp_out, vel_out, half, pos, pair, near_sum):
-    del half_in, pos_in, pair_in, sum_in
+def steps_kernel(coef, flow_in, pos_in, pair_in, sum_in, disp_out, vel_out, flow, pos, pair, near_sum):
+    del flow_in, pos_in, pair_in, sum_in
     k = 0
     while k < STEPS:
         first, last = region(k)
@@ -346,7 +378,7 @@
         def advance(step, carry, starting=k == 0, first=first, last=last):
             scale = jnp.where(step == 0, 0.5 * TIME_STEP, TIME_STEP).astype(F32) if starting else TIME_STEP
             for index in range(first, last, 2):
-                move(pos, pair, near_sum, push, half, scale, 8 * index, 16)
+                move(pos, pair, near_sum, flow, scale, 8 * index, 16)
             for index in range(first, last, 2):
                 spread(pos, 8 * index, 16)
             for index in range(first, last, 2):
@@ -359,21 +391,21 @@
         disp_out[component] = pos[component, 0, 0, OWN]
     first, last = region(STEPS)
     for index in range(first, last, 2):
-        move(pos, pair, near_sum, push, half, 0.5 * TIME_STEP, 8 * index, 16)
+        move(pos, pair, near_sum, flow, 0.5 * TIME_STEP, 8 * index, 16, last=True)
     for component in range(2):
-        vel_out[component] = half[component, 0, OWN]
-
-
-def run_steps(half, push, pos, coef, pair, near_sum):
+        vel_out[component] = flow[component, 0, OWN]
+
+
+def run_steps(flow, pos, coef, pair, near_sum):
     vmem = pl.BlockSpec(memory_space=pltpu.VMEM)
     out = jax.ShapeDtypeStruct((2, ROWS, COLS), F32)
-    arrays = (push, coef, half, pos, pair, near_sum)
+    arrays = (coef, flow, pos, pair, near_sum)
     return pl.pallas_call(
         steps_kernel,
-        out_shape=(out, out, *(pltpu.VMEM(shape, F32) for shape in (SUM, POS, PAIR, SUM))),
+        out_shape=(out, out, *(pltpu.VMEM(shape, F32) for shape in (FLOW, POS, PAIR, SUM))),
         in_specs=[vmem] * len(arrays),
         out_specs=(vmem,) * 6,
-        input_output_aliases={2: 2, 3: 3, 4: 4, 5: 5},
+        input_output_aliases={1: 2, 2: 3, 3: 4, 4: 5},
         compiler_params=pltpu.CompilerParams(vmem_limit_bytes=24 * 1024 * 1024),
         name="steps",
     )(*(pltpu.with_memory_space_constraint(a, pltpu.VMEM) for a in arrays))[:2]

time: 33.1 us -> 32.1 us (0.970)
  the two profiles are of different devices: /device:TPU:1 before, /device:TPU:7 now
where the time goes in v3:
time: 32.1 us; the launch traced here: 31.9 us
  Pallas kernels  31.3 us (98%)
  between operations  0.64 us (2%)
    pallas_call x1, Pallas kernels, exchange(): pl.pallas_call(functools.partial(exchange_kernel, shape_x, shape_y), out_...  23 us
    pallas_call x1, Pallas kernels, run_steps(): pl.pallas_call(steps_kernel, out_shape=(out, out, *(pltpu.VMEM(shape, F32...  8.26 us

profile of v3, /device:TPU:7, one launch (start us, length us, event | category | flops | bytes accessed | tf_op | source)
XLA Modules:
  0.0 31.9 jit_solution(7243007865572402464)
XLA Ops:
  0.6 23.0 %exchange.1 = (f32[4,2,128,128]{3,2,1,0:T(8,128)S(1)}, f32[2,4,2,128,128]{4,3,2,1,0:T(8,128)S(1)}, f32[14,2,128,128]{3,2,1,0:T(8,128)S(1)}, f32[14,2,2,128,128]{4,3,2,1,0:T(8,128)S(1)}, f32[2,2,128,128]{3,2,1,0:T(8,128)S(1)}) custom-call(f32[2,32,128]{2,1,0:T(8,128)} %disp.1, f32[2,32,128]{2,1,0:T(8,128)} %vel.1, f32[32,128]{1,0:T(8,128)} %stiff_own.1, ...), custom_call_target="tpu_custom_call" | custom-call | tf_op jit(solution)/shard_map/exchange/pallas_call | solution.py:340
  23.6 8.3 %steps.1 = (f32[2,32,128]{2,1,0:T(8,128)}, f32[2,32,128]{2,1,0:T(8,128)}, f32[4,2,128,128]{3,2,1,0:T(8,128)S(1)}, f32[2,4,2,128,128]{4,3,2,1,0:T(8,128)S(1)}, f3...) custom-call(f32[14,2,128,128]{3,2,1,0:T(8,128)S(1)} %get-tuple-eleme, ...), custom_call_target="tpu_custom_call", output_to_operand_aliasing={{2}: (1, {}), {3}: (2, {}), {4}: (3, {}), {5}: (4, {})} | custom-call | tf_op jit(solution)/shard_map/steps/pallas_call | solution.py:403

commit v4 on v3

--- a/solution.py
+++ b/solution.py
@@ -366,34 +366,39 @@
     return (18 + 3 * k) // 8, (109 - 3 * k) // 8 + 1
 
 
-def steps_kernel(coef, flow_in, pos_in, pair_in, sum_in, disp_out, vel_out, flow, pos, pair, near_sum):
+def steps_kernel(coef, flow_in, pos_in, pair_in, sum_in, disp_out, vel_out, flow, pos, pair, near_sum, sent):
     del flow_in, pos_in, pair_in, sum_in
+    leave = pltpu.make_async_copy(pos.at[:, 0, 0, OWN], disp_out, sent)
     k = 0
     while k < STEPS:
         first, last = region(k)
         end = k + 1
-        while end < STEPS and region(end) == (first, last):
+        while end < STEPS - 1 and region(end) == (first, last):
             end += 1
 
-        def advance(step, carry, starting=k == 0, first=first, last=last):
+        def advance(step, carry, starting=k == 0, ending=end == STEPS, first=first, last=last):
             scale = jnp.where(step == 0, 0.5 * TIME_STEP, TIME_STEP).astype(F32) if starting else TIME_STEP
             for index in range(first, last, 2):
                 move(pos, pair, near_sum, flow, scale, 8 * index, 16)
+            if ending:
+                leave.start()
             for index in range(first, last, 2):
                 spread(pos, 8 * index, 16)
             for index in range(first, last, 2):
                 forces(pos, coef, pair, near_sum, 8 * index, 16)
             return carry
 
-        lax.fori_loop(k, end, advance, 0)
+        if end == STEPS:
+            advance(k, 0)
+        else:
+            lax.fori_loop(k, end, advance, 0)
         k = end
-    for component in range(2):
-        disp_out[component] = pos[component, 0, 0, OWN]
     first, last = region(STEPS)
     for index in range(first, last, 2):
         move(pos, pair, near_sum, flow, 0.5 * TIME_STEP, 8 * index, 16, last=True)
     for component in range(2):
         vel_out[component] = flow[component, 0, OWN]
+    leave.wait()
 
 
 def run_steps(flow, pos, coef, pair, near_sum):
@@ -404,7 +409,8 @@
         steps_kernel,
         out_shape=(out, out, *(pltpu.VMEM(shape, F32) for shape in (FLOW, POS, PAIR, SUM))),
         in_specs=[vmem] * len(arrays),
-        out_specs=(vmem,) * 6,
+        out_specs=(pl.BlockSpec(memory_space=pltpu.HBM), *(vmem,) * 5),
+        scratch_shapes=[pltpu.SemaphoreType.DMA],
         input_output_aliases={1: 2, 2: 3, 3: 4, 4: 5},
         compiler_params=pltpu.CompilerParams(vmem_limit_bytes=24 * 1024 * 1024),
         name="steps",

time: 32.1 us -> 32.2 us (level)
  no operation moved by 1% of the time
where the time goes in v4:
time: 32.2 us; the launch traced here: 32 us
  Pallas kernels  31.3 us (97%)
  between operations  0.64 us (2%)
    pallas_call x1, Pallas kernels, exchange(): pl.pallas_call(functools.partial(exchange_kernel, shape_x, shape_y), out_...  23 us
    pallas_call x1, Pallas kernels, run_steps(): pl.pallas_call(steps_kernel, out_shape=(out, out, *(pltpu.VMEM(shape, F32...  8.35 us

profile of v4, /device:TPU:7, one launch (start us, length us, event | category | flops | bytes accessed | tf_op | source)
XLA Modules:
  0.0 32.0 jit_solution(14376439296672941970)
XLA Ops:
  0.6 23.0 %exchange.1 = (f32[4,2,128,128]{3,2,1,0:T(8,128)S(1)}, f32[2,4,2,128,128]{4,3,2,1,0:T(8,128)S(1)}, f32[14,2,128,128]{3,2,1,0:T(8,128)S(1)}, f32[14,2,2,128,128]{4,3,2,1,0:T(8,128)S(1)}, f32[2,2,128,128]{3,2,1,0:T(8,128)S(1)}) custom-call(f32[2,32,128]{2,1,0:T(8,128)} %disp.1, f32[2,32,128]{2,1,0:T(8,128)} %vel.1, f32[32,128]{1,0:T(8,128)} %stiff_own.1, ...), custom_call_target="tpu_custom_call" | custom-call | tf_op jit(solution)/shard_map/exchange/pallas_call | solution.py:340
  23.6 8.3 %steps.1 = (f32[2,32,128]{2,1,0:T(8,128)}, f32[2,32,128]{2,1,0:T(8,128)}, f32[4,2,128,128]{3,2,1,0:T(8,128)S(1)}, f32[2,4,2,128,128]{4,3,2,1,0:T(8,128)S(1)}, f3...) custom-call(f32[14,2,128,128]{3,2,1,0:T(8,128)S(1)} %get-tuple-eleme, ...), custom_call_target="tpu_custom_call", output_to_operand_aliasing={{2}: (1, {}), {3}: (2, {}), {4}: (3, {}), {5}: (4, {})} | custom-call | tf_op jit(solution)/shard_map/steps/pallas_call | solution.py:408
